TPU v7x, 32 devices: a whole 2x2x4 slice. The times are simulated.
32 devices in a mesh: seq: 16 (over z, x, core), fsdp: 2 (over y).
Axes of the slice: x: 2, y: 2, z: 4, core: 2. Of those that a mesh axis runs over, the one named last changes fastest.
Arguments:
- tokens: bfloat16 [2, 4096, 1024], P('fsdp', 'seq'), may hold values from -6 to 6
- cotangent: bfloat16 [2, 4096, 1024], P('fsdp', 'seq'), may hold values from -6 to 6
- seq_lengths: int32 [2, 3], replicated, may hold values from 1 to 3840, as said below
- group_of_shard: int32 [2], replicated, may hold values from 0 to 1, each once
- gain_attn: bfloat16 [1024], P('fsdp'), may hold values from 0.5 to 1.5
- w_query: bfloat16 [1024, 1024], P('fsdp'), may hold values from -0.1875 to 0.1875
- w_key: bfloat16 [1024, 128], P('fsdp'), may hold values from -0.1875 to 0.1875
- w_value: bfloat16 [1024, 128], P('fsdp'), may hold values from -0.1875 to 0.1875
- w_out: bfloat16 [1024, 1024], P('fsdp'), may hold values from -3 to 3
- gain_ffn: bfloat16 [1024], P('fsdp'), may hold values from 0.5 to 1.5
- w_up: bfloat16 [1024, 4096], P('fsdp'), may hold values from -0.1875 to 0.1875
- w_down: bfloat16 [4096, 1024], P('fsdp'), may hold values from -0.09375 to 0.09375
Outputs:
- output: bfloat16 [2, 4096, 1024], P('fsdp', 'seq')
- grad_tokens: float32 [2, 4096, 1024], P('fsdp', 'seq')
- grad_gain_attn: float32 [1024], P('fsdp')
- grad_w_query: float32 [1024, 1024], P('fsdp')
- grad_w_key: float32 [1024, 128], P('fsdp')
- grad_w_value: float32 [1024, 128], P('fsdp')
- grad_w_out: float32 [1024, 1024], P('fsdp')
- grad_gain_ffn: float32 [1024], P('fsdp')
- grad_w_up: float32 [1024, 4096], P('fsdp')
- grad_w_down: float32 [4096, 1024], P('fsdp')
Inputs may be any that keep to these rules, and one draw needn't show every extreme that they name: `seq_lengths`: row g lists the lengths of the 3 sequences of group g in the order in which they are packed; the middle one is exactly 3840, the first and the last add up to 256. `group_of_shard`: each group appears once.
All inputs are finite; a program needn't handle non-finite values.
Results may differ from a plain program's by a relative error of at most 0.015.
Values may be sent and summed in bfloat16 or wider, within the bound.
A program may use at most 192 MiB of HBM per device.

v0:
```python
import functools
import math
import types

import jax
import jax.numpy as jnp
from jax import lax
from jax.experimental import pallas as pl
from jax.experimental.pallas import tpu as pltpu
from jax.sharding import PartitionSpec as P

H = 8
HS = 128
EPS = 1e-05
NEG = -1e30
LIMIT = 60 * 2**20
CHUNK = 512
BF = jnp.bfloat16
F32 = jnp.float32


def nt(a, b):
    return lax.dot_general(a, b, (((1,), (1,)), ((), ())), preferred_element_type=F32)


def nn(a, b):
    return lax.dot_general(a, b, (((1,), (0,)), ((), ())), preferred_element_type=F32)


def tn(a, b):
    return lax.dot_general(a, b, (((0,), (0,)), ((), ())), preferred_element_type=F32)


def query_range(scal, tok):
    first = scal[0] * tok
    pos = first + lax.broadcasted_iota(jnp.int32, (1, tok), 1)
    start = jnp.zeros((1, tok), jnp.int32)
    latest = jnp.int32(0)
    for i in range(1, scal.shape[0]):
        end = scal[i]
        start = jnp.maximum(start, jnp.where(end <= pos, end, 0))
        latest = jnp.maximum(latest, jnp.where(end <= first + tok - 1, end, 0))
    return first, pos, start, latest


def chunk_loop(scal, tok, window, step):
    first, pos, start, latest = query_range(scal, tok)
    chunks = (first + tok + CHUNK - 1) // CHUNK

    def body(j, carry):
        low = j * CHUNK
        whole = jnp.logical_and(low >= latest, low + CHUNK - 1 <= first)

        @pl.when(whole)
        def _():
            step(j, None)

        @pl.when(jnp.logical_not(whole))
        def _():
            keys = low + lax.broadcasted_iota(jnp.int32, (CHUNK, tok), 0)
            step(j, jnp.logical_and(keys >= start, keys <= pos))

        return carry

    lax.fori_loop(0, chunks, body, 0)
    return chunks


def attend_kernel(scal, q_ref, kv_ref, out_ref, lse_ref, acc, top, total):
    tok = q_ref.shape[0]
    factor = math.log2(math.e) / math.sqrt(HS)
    top[...] = jnp.full(top.shape, -3e38, F32)
    total[...] = jnp.zeros(total.shape, F32)
    acc[...] = jnp.zeros(acc.shape, F32)

    def step(j, mask):
        rows = pl.ds(pl.multiple_of(j * CHUNK, CHUNK), CHUNK)
        keys = kv_ref[rows, :HS]
        values_t = kv_ref[rows, HS:].T
        for h in range(H):
            scores = nt(keys, q_ref[:, h * HS : (h + 1) * HS])
            if mask is not None:
                scores = jnp.where(mask, scores, NEG)
            old = top[h : h + 1, :]
            new = jnp.maximum(old, jnp.max(scores, axis=0, keepdims=True) * factor)
            shrink = jnp.exp2(old - new)
            probs = jnp.exp2(scores * factor - new)
            total[h : h + 1, :] = total[h : h + 1, :] * shrink + jnp.sum(probs, axis=0, keepdims=True)
            acc[h] = acc[h] * shrink + nn(values_t, probs.astype(BF))
            top[h : h + 1, :] = new

    chunk_loop(scal, tok, kv_ref.shape[0], step)
    for h in range(H):
        mixed = acc[h] * (1.0 / total[h : h + 1, :])
        out_ref[:, h * HS : (h + 1) * HS] = mixed.T.astype(BF)
    lse_ref[...] = top[...] + jnp.log2(total[...])


VMEM = pl.BlockSpec(memory_space=pltpu.VMEM)
SMEM = pl.BlockSpec(memory_space=pltpu.SMEM)
PARAMS = pltpu.CompilerParams(vmem_limit_bytes=40 * 2**20)


def attend(scal, queries, window_kv):
    tok = queries.shape[0]
    window = window_kv.shape[0]
    return pl.pallas_call(
        attend_kernel,
        out_shape=(
            jax.ShapeDtypeStruct((tok, H * HS), BF),
            jax.ShapeDtypeStruct((H, tok), F32),
        ),
        in_specs=[SMEM, VMEM, VMEM],
        out_specs=(VMEM, VMEM),
        scratch_shapes=[
            pltpu.VMEM((H, HS, tok), F32),
            pltpu.VMEM((H, tok), F32),
            pltpu.VMEM((H, tok), F32),
        ],
        compiler_params=PARAMS,
        cost_estimate=pl.CostEstimate(
            flops=8 * tok * window * H * HS, bytes_accessed=4 * window * HS, transcendentals=tok * window * H
        ),
        name="attend",
    )(scal, queries, window_kv)


MESH = pl.DeviceIdType.MESH


TAIL_IN = (
    "ends",
    "q_ref",
    "kv_ref",
    "d_ref",
    "att_ref",
    "lse_ref",
    "gd_ref",
    "gu_ref",
    "go_ref",
    "n1_ref",
    "wq_ref",
    "wkv_ref",
    "tok_ref",
    "inv_ref",
    "gain_ref",
    "dres_ref",
    "gain2_ref",
)
TAIL_OUT = (
    "out_down",
    "out_up",
    "out_o",
    "out_q",
    "out_kv",
    "grad_tokens",
)
TAIL_SCRATCH = (
    "acc",
    "delta",
    "dq",
    "dkv",
    "dkv_c",
    "dkv_x",
    "dkv_z",
    "d_kv",
    "dn1",
    "gq_ref",
    "gkv_ref",
    "xr_d",
    "xr_u",
    "zs_d",
    "zs_u",
    "zr_d",
    "zr_u",
    "sh_d",
    "sh_u",
    "yr_u",
    "o_c",
    "o_y",
    "o_x",
    "o_z",
    "o_s",
    "q_c",
    "q_y",
    "q_x",
    "q_z",
    "q_s",
    "kv_c",
    "kv_y",
    "kv_x",
    "kv_z",
    "kv_s",
    "gain_rows",
    "send_sem",
    "recv_sem",
    "copy_sem",
)


def tail_kernel(dims, head, names, *refs):
    A, B, F = dims
    r = types.SimpleNamespace(**dict(zip(names, refs, strict=True)))
    if head is not None:
        for name, held in AGAIN.items():
            setattr(r, name, getattr(r, held))
    ends = r.ends
    q_ref = r.q_ref
    kv_ref = r.kv_ref
    d_ref = r.d_ref
    att_ref = r.att_ref
    lse_ref = r.lse_ref
    gd_ref = r.gd_ref
    gu_ref = r.gu_ref
    go_ref = r.go_ref
    n1_ref = r.n1_ref
    wq_ref = r.wq_ref
    wkv_ref = r.wkv_ref
    tok_ref = r.tok_ref
    inv_ref = r.inv_ref
    gain_ref = r.gain_ref
    dres_ref = r.dres_ref
    gain2_ref = r.gain2_ref
    out_down = r.out_down
    out_up = r.out_up
    out_o = r.out_o
    out_q = r.out_q
    out_kv = r.out_kv
    grad_tokens = r.grad_tokens
    acc = r.acc
    delta = r.delta
    dq = r.dq
    dkv = r.dkv
    dkv_c = r.dkv_c
    dkv_x = r.dkv_x
    dkv_z = r.dkv_z
    d_kv = r.d_kv
    dn1 = r.dn1
    gq_ref = r.gq_ref
    gkv_ref = r.gkv_ref
    xr_d = r.xr_d
    xr_u = r.xr_u
    zs_d = r.zs_d
    zs_u = r.zs_u
    zr_d = r.zr_d
    zr_u = r.zr_u
    sh_d = r.sh_d
    sh_u = r.sh_u
    yr_u = r.yr_u
    o_c = r.o_c
    o_y = r.o_y
    o_x = r.o_x
    o_z = r.o_z
    o_s = r.o_s
    q_c = r.q_c
    q_y = r.q_y
    q_x = r.q_x
    q_z = r.q_z
    q_s = r.q_s
    kv_c = r.kv_c
    kv_y = r.kv_y
    kv_x = r.kv_x
    kv_z = r.kv_z
    kv_s = r.kv_s
    gain_rows = r.gain_rows
    send_sem = r.send_sem
    recv_sem = r.recv_sem
    copy_sem = r.copy_sem
    tok = q_ref.shape[0]
    window = kv_ref.shape[0]
    D = n1_ref.shape[1]
    own_rows = D // F
    shard = gd_ref.shape[0]
    s = lax.axis_index("seq")
    f = lax.axis_index("fsdp")
    c = lax.rem(s, 2)
    b = lax.rem(s // 2, B)
    a = s // (2 * B)

    def device(axis, step):
        at = {"a": a, "b": b, "c": c, "f": f}
        at[axis] = lax.rem(at[axis] + step, {"a": A, "b": B, "c": 2, "f": F}[axis])
        return ((at["a"] * B + at["b"]) * 2 + at["c"], at["f"])

    def lower(axis, step):
        return lax.rem({"a": a + A, "b": b + B, "f": f + F}[axis] - step, {"a": A, "b": B, "f": F}[axis])

    used = [0]

    def slots(n=1):
        used[0] += n
        assert used[0] <= send_sem.shape[0]
        return used[0] - n

    def remote(src, dst, slot, to):
        return pltpu.make_async_remote_copy(
            src_ref=src, dst_ref=dst, send_sem=send_sem.at[slot], recv_sem=recv_sem.at[slot], device_id=to, device_id_type=MESH
        )

    pending = []

    def start(src, dst, slot, to):
        copy = remote(src, dst, slot, to)
        copy.start()
        pending.append(copy)
        return copy

    barrier = pltpu.get_barrier_semaphore()
    partners = [("a", k) for k in range(1, A)] + [("b", k) for k in range(1, B)] + [("c", 1)] + [("f", k) for k in range(1, F)]
    for axis, k in partners:
        pl.semaphore_signal(barrier, inc=1, device_id=device(axis, k), device_id_type=MESH)
    pl.semaphore_wait(barrier, len(partners))

    r_d = shard // (A * B)
    r_u = own_rows // B
    w_u = shard // A
    x_d = slots(A * (B - 1))
    x_u = slots(A * (B - 1))
    z_d = slots(A - 1)
    z_u = slots(A - 1)

    def down_copies(i):
        at = lax.rem(a + 1 + i, A)
        copies = []
        for kb in range(B - 1):
            other = lax.rem(b + kb + 1, B)
            rows = pl.ds(pl.multiple_of((other * A + at) * r_d, r_d), r_d)
            copies.append(remote(gd_ref.at[rows, :], xr_d.at[kb, i], x_d + kb * A + i, device("b", kb + 1)))
        return copies

    def up_copies(i):
        at = lax.rem(a + 1 + i, A)
        copies = []
        for kb in range(B - 1):
            rows = pl.ds(pl.multiple_of(lax.rem(b + kb + 1, B) * r_u, r_u), r_u)
            cols = pl.ds(pl.multiple_of(at * w_u, w_u), w_u)
            copies.append(remote(gu_ref.at[:, rows, cols], xr_u.at[kb, i], x_u + kb * A + i, device("b", kb + 1)))
        return copies

    def send_down(first, last):
        for i in range(first, last):
            for copy in down_copies(i):
                copy.start()

    def send_up(first, last):
        for i in range(first, last):
            for copy in up_copies(i):
                copy.start()

    def own_sums(i):
        at = lax.rem(a + 1 + i, A)
        rows = pl.ds(pl.multiple_of((b * A + at) * r_d, r_d), r_d)
        total_d = gd_ref[rows, :].astype(F32)
        rows = pl.ds(pl.multiple_of(b * r_u, r_u), r_u)
        cols = pl.ds(pl.multiple_of(at * w_u, w_u), w_u)
        total_u = gu_ref[:, rows, cols].astype(F32)
        for kb in range(B - 1):
            total_d = total_d + xr_d[kb, i].astype(F32)
            total_u = total_u + xr_u[kb, i].astype(F32)
        return total_d, total_u

    if head is None:
        for i in range(A):
            send_down(i, i + 1)
            send_up(i, i + 1)
    else:
        own = types.SimpleNamespace(
            A=A, B=B, F=F, a=a, b=b, c=c, f=f, s=s, slots=slots, remote=remote, device=device, lower=lower,
            send_down=send_down, send_up=send_up,
        )
        finish_output, finish_head = head(r, own)

    half = D // 2

    def reduce_c(ref, got, width):
        other = pl.ds(pl.multiple_of((1 - c) * width, width), width)
        return start(ref.at[:, :, other], got, slots(), device("c", 1))

    def reduce_y(ref, got, sent, width):
        mine = pl.ds(pl.multiple_of(c * width, width), width)

        def add(i, carry):
            sent[i] = (ref[i, :, mine].astype(F32) + got[i].astype(F32)).astype(BF)
            return carry

        lax.fori_loop(0, F, add, 0)

    o_c_copy = reduce_c(go_ref, o_c, half)

    scale = 1.0 / math.sqrt(HS)
    factor = math.log2(math.e) * scale
    acc[...] = jnp.zeros(acc.shape, F32)
    for h in range(H):
        cols = slice(h * HS, (h + 1) * HS)
        both = d_ref[:, cols].astype(F32) * att_ref[:, cols].astype(F32)
        delta[h : h + 1, :] = jnp.sum(both.T, axis=0, keepdims=True)
    first = s * tok
    pos = first + lax.broadcasted_iota(jnp.int32, (1, tok), 1)
    begin = jnp.zeros((1, tok), jnp.int32)
    for i in range(ends.shape[0]):
        begin = jnp.maximum(begin, jnp.where(ends[i] <= pos, ends[i], 0))

    def step(j, masked):
        rows = pl.ds(pl.multiple_of(j * CHUNK, CHUNK), CHUNK)
        keys = kv_ref[rows, :HS]
        values = kv_ref[rows, HS:]
        keys_t = keys.T
        if masked:
            at = j * CHUNK + lax.broadcasted_iota(jnp.int32, (CHUNK, tok), 0)
            mask = jnp.logical_and(at >= begin, at <= pos)
        d_keys = jnp.zeros((CHUNK, HS), F32)
        d_values = jnp.zeros((CHUNK, HS), F32)
        for h in range(H):
            cols = slice(h * HS, (h + 1) * HS)
            q = q_ref[:, cols]
            d = d_ref[:, cols]
            scores = nt(keys, q)
            if masked:
                scores = jnp.where(mask, scores, NEG)
            probs = jnp.exp2(scores * factor - lse_ref[h : h + 1, :])
            d_probs = nt(values, d)
            d_scores = (probs * (d_probs - delta[h : h + 1, :])).astype(BF)
            d_values = d_values + nn(probs.astype(BF), d)
            d_keys = d_keys + nn(d_scores, q)
            acc[h] = acc[h] + nn(keys_t, d_scores)
        for i in range(2):
            part = slice(i * tok, (i + 1) * tok)
            dkv[j, i, :, :HS] = (d_keys[part] * scale).astype(BF)
            dkv[j, i, :, HS:] = d_values[part].astype(BF)

    chunks = s // 2 + 1
    per = -(-(window // CHUNK) // max(1, A - 1))

    def attention_chunk(j, carry):
        plain = jnp.logical_and(jnp.logical_and(j > 0, j < chunks - 1), s < 2 * A * B - 1)

        @pl.when(plain)
        def _():
            step(j, False)

        @pl.when(jnp.logical_not(plain))
        def _():
            step(j, True)

        return carry

    def feed_forward_step(i, carry):
        lax.fori_loop(i * per, jnp.minimum((i + 1) * per, chunks), attention_chunk, 0)
        for copy in down_copies(i) + up_copies(i):
            copy.wait()
        total_d, total_u = own_sums(i)
        to = lax.rem(a + 1 + i, A)
        to = ((to * B + b) * 2 + c, f)
        zs_d[i] = total_d.astype(BF)
        remote(zs_d.at[i], zr_d.at[i], z_d + i, to).start()
        zs_u[i] = total_u.astype(BF)
        remote(zs_u.at[i], zr_u.at[i], z_u + i, to).start()
        return carry

    lax.fori_loop(0, A - 1, feed_forward_step, 0)

    def clear(j, carry):
        dkv[j] = jnp.zeros(dkv.shape[1:], BF)
        return carry

    lax.fori_loop(chunks, window // CHUNK, clear, 0)

    class Gather:
        def __init__(self, share, view, planes=True):
            self.share, self.view, self.planes = share, view, planes
            n = B if planes else 1
            self.z = slots(A - 1)
            self.x = slots((n - 1) * A)
            self.s = slots(n * A)
            self.local = pltpu.make_async_copy(share, view(c, b, a), copy_sem.at[len(gathers)])
            gathers.append(self)

        def begin(self):
            self.local.start()
            mine = self.view(c, b, a)
            self.zs = [start(self.share, mine, self.z + k, device("a", k + 1)) for k in range(A - 1)]
            self.xs, self.cs = {}, {}
            self.pass_on(self.share, mine, 0)

        def pass_on(self, src, dst, j):
            for kb in range(B - 1 if self.planes else 0):
                self.xs[kb, j] = start(src, dst, self.x + kb * A + j, device("b", kb + 1))
            self.cs[0, j] = start(src, dst, self.s + j, device("c", 1))

        def from_a(self):
            for k in range(A - 1):
                self.zs[k].wait_recv()
                here = self.view(c, b, lower("a", k + 1))
                self.pass_on(here, here, k + 1)

        def from_b(self):
            for kb in range(B - 1 if self.planes else 0):
                for j in range(A):
                    self.xs[kb, j].wait_recv()
                    here = self.view(c, lower("b", kb + 1), lower("a", j) if j else a)
                    self.cs[kb + 1, j] = start(here, here, self.s + (kb + 1) * A + j, device("c", 1))

        def end(self):
            self.local.wait()
            for copy in self.zs + list(self.xs.values()):
                copy.wait_send()
            for copy in self.cs.values():
                copy.wait()

    gathers = []

    def view_down(c_, b_, a_):
        return out_down.at[pl.ds(pl.multiple_of(((c_ * B + b_) * A + a_) * r_d, r_d), r_d), :]

    def view_up(c_, b_, a_):
        rows = pl.ds(pl.multiple_of(b_ * r_u, r_u), r_u)
        return out_up.at[:, rows, pl.ds(pl.multiple_of(c_ * shard + a_ * w_u, w_u), w_u)]

    w_o = half // A

    def view_square(out):
        def view(c_, b_, a_):
            rows = pl.ds(pl.multiple_of(b_ * r_u, r_u), r_u)
            return out.at[rows, pl.ds(pl.multiple_of(c_ * half + a_ * w_o, w_o), w_o)]

        return view

    gather_down = Gather(sh_d, view_down)
    gather_up = Gather(sh_u, view_up)
    gather_o = Gather(o_s, view_square(out_o))
    gather_q = Gather(q_s, view_square(out_q))
    gather_kv = Gather(kv_s, lambda c_, b_, a_: out_kv.at[c_, a_], planes=False)

    dkv_c_copy = start(dkv.at[:, 1 - c], dkv_c, slots(), device("c", 1))

    for copy in down_copies(A - 1) + up_copies(A - 1):
        copy.wait()
    total_d, total_u = own_sums(A - 1)

    def z_wait(i, carry):
        to = lax.rem(a + 1 + i, A)
        to = ((to * B + b) * 2 + c, f)
        remote(zs_d.at[i], zr_d.at[i], z_d + i, to).wait()
        remote(zs_u.at[i], zr_u.at[i], z_u + i, to).wait()
        return carry

    lax.fori_loop(0, A - 1, z_wait, 0)
    for i in range(A - 1):
        total_d = total_d + zr_d[i].astype(F32)
        total_u = total_u + zr_u[i].astype(F32)
    sh_d[...] = total_d.astype(BF)
    gather_down.begin()
    yr_u[...] = total_u.astype(BF)
    up_y = []
    for kf in range(F - 1):
        up_y.append(start(yr_u.at[lax.rem(f + kf + 1, F)], sh_u.at[f], slots(), device("f", kf + 1)))
    sh_u[f] = yr_u[f]

    class Square:
        def __init__(self, grad, got_c, got_y, got_x, got_z, share, gather):
            self.grad, self.got_c, self.got_y, self.got_x, self.got_z = grad, got_c, got_y, got_x, got_z
            self.share, self.gather = share, gather

        def over_c(self):
            self.copy_c = reduce_c(self.grad, self.got_c, half)

        def over_f(self):
            self.copy_c.wait()
            reduce_y(self.grad, self.got_c, self.got_c, half)
            self.copies = [
                start(self.got_c.at[lax.rem(f + kf + 1, F)], self.got_y.at[kf], slots(), device("f", kf + 1)) for kf in range(F - 1)
            ]

        def over_b(self):
            total = self.got_c[f].astype(F32)
            for kf in range(F - 1):
                self.copies[kf].wait()
                total = total + self.got_y[kf].astype(F32)
            self.got_y[F - 1] = total.astype(BF)
            self.copies = []
            for kb in range(B - 1):
                rows = pl.ds(pl.multiple_of(lax.rem(b + kb + 1, B) * r_u, r_u), r_u)
                self.copies.append(start(self.got_y.at[F - 1, rows, :], self.got_x.at[kb], slots(), device("b", kb + 1)))

        def over_a(self):
            rows = pl.ds(pl.multiple_of(b * r_u, r_u), r_u)
            total = self.got_y[F - 1, rows, :].astype(F32)
            for kb in range(B - 1):
                self.copies[kb].wait()
                total = total + self.got_x[kb].astype(F32)
            self.got_x[B - 1] = total.astype(BF)
            self.copies = []
            for ka in range(A - 1):
                cols = pl.ds(pl.multiple_of(lax.rem(a + ka + 1, A) * w_o, w_o), w_o)
                self.copies.append(start(self.got_x.at[B - 1, :, cols], self.got_z.at[ka], slots(), device("a", ka + 1)))

        def finish(self):
            cols = pl.ds(pl.multiple_of(a * w_o, w_o), w_o)
            total = self.got_x[B - 1, :, cols].astype(F32)
            for ka in range(A - 1):
                self.copies[ka].wait()
                total = total + self.got_z[ka].astype(F32)
            self.share[...] = total.astype(BF)
            self.gather.begin()

    square_o = Square(go_ref, o_c, o_y, o_x, o_z, o_s, gather_o)
    square_o.copy_c = o_c_copy
    square_q = Square(gq_ref, q_c, q_y, q_x, q_z, q_s, gather_q)

    square_o.over_f()

    if head is not None:
        finish_output()
    for h in range(H):
        dq[:, h * HS : (h + 1) * HS] = (acc[h] * scale).T.astype(BF)
    n_rows = 128

    def query_grad(i, carry):
        col = pl.ds(pl.multiple_of(i * n_rows, n_rows), n_rows)
        fi = i // (own_rows // n_rows)
        row = lax.rem(i, own_rows // n_rows) * n_rows
        gq_ref[fi, pl.ds(pl.multiple_of(row, n_rows), n_rows), :] = nn(n1_ref[:, col].T, dq[...]).astype(BF)
        return carry

    lax.fori_loop(0, D // n_rows, query_grad, 0)
    square_q.over_c()

    dkv_c_copy.wait()

    def add_c(j, carry):
        dkv_c[j] = (dkv_c[j].astype(F32) + dkv[j, c].astype(F32)).astype(BF)
        return carry

    lax.fori_loop(0, A * B, add_c, 0)
    x_kv = []
    for kb in range(B - 1):
        other = lax.rem(b + kb + 1, B)
        for j in range(A):
            x_kv.append(start(dkv_c.at[j * B + other], dkv_x.at[kb, j], slots(), device("b", kb + 1)))

    square_o.over_b()
    for copy in up_y:
        copy.wait()
    gather_up.begin()
    gather_down.from_a()
    square_q.over_f()

    for copy in x_kv:
        copy.wait()

    def add_x(j, carry):
        total = dkv_c[j * B + b].astype(F32)
        for kb in range(B - 1):
            total = total + dkv_x[kb, j].astype(F32)
        dkv_x[0, j] = total.astype(BF)
        return carry

    lax.fori_loop(0, A, add_x, 0)
    z_kv = slots(A - 1)
    for k in range(1, A):

        @pl.when(a - k >= 0)
        def _():
            to = (((a - k) * B + b) * 2 + c, f)
            remote(dkv_x.at[0, jnp.maximum(a - k, 0)], dkv_z.at[k - 1], z_kv + k - 1, to).start()

    square_o.over_a()
    square_q.over_b()
    gather_up.from_a()

    total = dkv_x[0, a].astype(F32)
    d_kv[...] = total
    for k in range(1, A):
        copy = remote(dkv_x.at[0, jnp.maximum(a - k, 0)], dkv_z.at[k - 1], z_kv + k - 1, device("a", A - k))

        @pl.when(a - k >= 0)
        def _():
            copy.wait_send()

        @pl.when(a + k < A)
        def _():
            copy.wait_recv()
            d_kv[...] = d_kv[...] + dkv_z[k - 1].astype(F32)

    d_kv_low = d_kv[...].astype(BF)

    n_cols = 256
    mean = jnp.zeros((tok, 1), F32)
    for i in range(D // n_cols):
        cols = slice(i * n_cols, (i + 1) * n_cols)
        part = nt(dq[...], wq_ref[cols, :]) + nt(d_kv_low, wkv_ref[cols, :])
        dn1[:, cols] = part
        weighted = part * (tok_ref[:, cols].astype(F32) * inv_ref[...])
        gain_rows[0:1, cols] = jnp.sum(weighted, axis=0, keepdims=True)
        mean = mean + jnp.sum(weighted * gain_ref[:, cols], axis=1, keepdims=True)
    if head is None:
        gain_rows[1:2, :] = gain2_ref[...]
    mean = mean * (1.0 / D)

    r_kv = own_rows // A
    rows_kv = r_kv + 16
    for fi in range(F):
        for i in range(A):
            at = fi * own_rows + i * r_kv
            part = tn(n1_ref[:, at : at + r_kv], d_kv_low).astype(BF)
            gkv_ref[0, fi, i, :r_kv, :] = part[:, :HS]
            gkv_ref[1, fi, i, :r_kv, :] = part[:, HS:]
            for ci in range(2):
                rows = [gain_rows[ci : ci + 1, fi * own_rows + k * 128 : fi * own_rows + (k + 1) * 128] for k in range(own_rows // 128)]
                block = jnp.concatenate(rows + [jnp.zeros((16 - len(rows), 128), F32)], axis=0)
                gkv_ref[ci, fi, i, r_kv:, :] = block.astype(BF)
    kv_c_copy = start(gkv_ref.at[1 - c], kv_c, slots(), device("c", 1))

    square_o.finish()
    for i in range(D // n_cols):
        cols = slice(i * n_cols, (i + 1) * n_cols)
        grad_tokens[:, cols] = dres_ref[:, cols] + inv_ref[...] * (
            dn1[:, cols] * gain_ref[:, cols] - tok_ref[:, cols].astype(F32) * inv_ref[...] * mean
        )
    square_q.over_a()
    kv_c_copy.wait()
    kv_c[...] = (kv_c[...].astype(F32) + gkv_ref[c].astype(F32)).astype(BF)
    kv_f = [start(kv_c.at[lax.rem(f + kf + 1, F)], kv_y.at[kf], slots(), device("f", kf + 1)) for kf in range(F - 1)]
    gather_down.from_b()
    gather_o.from_a()
    total = kv_c[f].astype(F32)
    for kf in range(F - 1):
        kv_f[kf].wait()
        total = total + kv_y[kf].astype(F32)
    kv_y[F - 1] = total.astype(BF)
    kv_b = [start(kv_y.at[F - 1], kv_x.at[kb], slots(), device("b", kb + 1)) for kb in range(B - 1)]
    square_q.finish()
    total = kv_y[F - 1].astype(F32)
    for kb in range(B - 1):
        kv_b[kb].wait()
        total = total + kv_x[kb].astype(F32)
    kv_x[B - 1] = total.astype(BF)
    kv_a = [start(kv_x.at[B - 1, lax.rem(a + ka + 1, A)], kv_z.at[ka], slots(), device("a", ka + 1)) for ka in range(A - 1)]
    gather_up.from_b()
    total = kv_x[B - 1, a].astype(F32)
    for ka in range(A - 1):
        kv_a[ka].wait()
        total = total + kv_z[ka].astype(F32)
    kv_s[...] = total.astype(BF)
    gather_kv.begin()
    gather_q.from_a()
    gather_o.from_b()
    gather_kv.from_a()
    gather_q.from_b()
    for gather in gathers:
        gather.end()
    if head is not None:
        finish_head()


def tail_shapes(dims, tok, D, shard, window, extra):
    A, B, F = dims
    own_rows = D // F
    half, r_d, r_u, w_u = D // 2, shard // (A * B), own_rows // B, shard // A
    w_o, r_kv = half // A, own_rows // A + 16

    def low(*shape):
        return pltpu.VMEM(shape, BF)

    square = [low(F, own_rows, half), low(F, own_rows, half), low(B, r_u, half), low(A - 1, r_u, w_o), low(r_u, w_o)]
    n_sems = extra + 2 * (A * (B - 1) + A - 1) + 4 * (A - 1 + (B - 1) * A + B * A) + (A - 1 + A)
    n_sems += 2 * (F + B + A) + F + (B - 1) * A + A + F + B + A + 8
    outs = (
        jax.ShapeDtypeStruct((2 * shard, D), BF),
        jax.ShapeDtypeStruct((F, own_rows, 2 * shard), BF),
        jax.ShapeDtypeStruct((own_rows, D), BF),
        jax.ShapeDtypeStruct((own_rows, D), BF),
        jax.ShapeDtypeStruct((2, A, r_kv, HS), BF),
        jax.ShapeDtypeStruct((tok, D), F32),
    )
    scratch = [
        pltpu.VMEM((H, HS, tok), F32),
        pltpu.VMEM((H, tok), F32),
        low(tok, D),
        low(A * B, 2, tok, 2 * HS),
        low(A * B, tok, 2 * HS),
        low(max(1, B - 1), A, tok, 2 * HS),
        low(max(1, A - 1), tok, 2 * HS),
        pltpu.VMEM((tok, 2 * HS), F32),
        pltpu.VMEM((tok, D), F32),
        low(F, own_rows, D),
        low(2, F, A, r_kv, HS),
        low(B - 1, A, r_d, D),
        low(B - 1, A, F, r_u, w_u),
        low(A - 1, r_d, D),
        low(A - 1, F, r_u, w_u),
        low(A - 1, r_d, D),
        low(A - 1, F, r_u, w_u),
        low(r_d, D),
        low(F, r_u, w_u),
        low(F, r_u, w_u),
        *square,
        *square,
        low(F, A, r_kv, HS),
        low(F, A, r_kv, HS),
        low(B, A, r_kv, HS),
        low(A - 1, r_kv, HS),
        low(r_kv, HS),
        pltpu.VMEM((8, D), F32),
        pltpu.SemaphoreType.DMA((n_sems,)),
        pltpu.SemaphoreType.DMA((n_sems,)),
        pltpu.SemaphoreType.DMA((5,)),
    ]
    return outs, scratch


def tail(dims, ends, queries, window_kv, d_attended, attended, lse, grad_down, grad_up, grad_out, n1, wq, wkv, tokens, inv, gain, dres, gain2):
    A, B, F = dims
    tok, D = n1.shape
    window = window_kv.shape[0]
    outs, scratch = tail_shapes(dims, tok, D, grad_down.shape[0], window, 0)
    hbm = pl.BlockSpec(memory_space=pltpu.HBM)
    return pl.pallas_call(
        functools.partial(tail_kernel, dims, None, TAIL_IN + TAIL_OUT + TAIL_SCRATCH),
        out_shape=outs,
        in_specs=[SMEM] + [VMEM] * 16,
        out_specs=(hbm,) * 5 + (VMEM,),
        scratch_shapes=scratch,
        compiler_params=pltpu.CompilerParams(vmem_limit_bytes=56 * 2**20, collective_id=1, has_side_effects=True),
        cost_estimate=pl.CostEstimate(flops=20 * tok * window * D, bytes_accessed=2**25, transcendentals=tok * window * H),
        name="tail",
    )(ends, queries, window_kv, d_attended, attended, lse, grad_down, grad_up, grad_out, n1, wq, wkv, tokens, inv, gain, dres, gain2)


HEAD_IN = (
    "ends",
    "tokens",
    "gains_in",
    "wk_in",
    "wv_in",
    "cot_in",
    "wq_in",
    "wo_in",
    "up_in",
    "down_in",
)
HEAD_SCRATCH = (
    "q_ref",
    "kv_ref",
    "d_ref",
    "att_ref",
    "lse_ref",
    "gd_ref",
    "gu_ref",
    "n1_ref",
    "wq_ref",
    "wkv_ref",
    "inv_ref",
    "gain_ref",
    "dres_ref",
    "gain2_ref",
    "wo_ref",
    "up_ref",
    "down_ref",
    "gains_all",
    "cot_all",
    "n2_all",
    "hid_all",
    "dp_all",
    "res_ref",
    "inv2_ref",
    "dbr_ref",
    "back_s",
    "back_c",
    "back_y",
    "back_r",
    "out_s",
    "out_c",
    "out_y",
    "out_r",
    "top",
    "total",
    "loc_sem",
)


def head(r, x):
    A, B, F, a, b, c, f, s = x.A, x.B, x.F, x.a, x.b, x.c, x.f, x.s
    slots, remote, device, lower = x.slots, x.remote, x.device, x.lower
    tok, D = r.tokens.shape
    own_rows = D // F
    shard = r.down_ref.shape[0]
    half = own_rows // 2
    sent = []

    def start(src, dst, to, slot=None):
        copy = remote(src, dst, slots() if slot is None else slot, to)
        copy.start()
        sent.append(copy)
        return copy

    def done(copies):
        for copy in copies:
            copy.wait_send()
            sent[:] = [other for other in sent if other is not copy]

    def span(at, n):
        return pl.ds(pl.multiple_of(at, n), n)

    sibling = device("c", 1)
    mine, mine_half = span(f * own_rows, own_rows), span(c * half, half)
    full_half = span((f * 2 + c) * half, half)

    def to_f(src, dst):
        return [start(src(kf), dst(kf), device("f", kf)) for kf in range(1, F)]

    gains_f = to_f(lambda kf: r.gains_in, lambda kf: r.gains_all.at[f])
    wk_f = to_f(lambda kf: r.wk_in.at[mine_half, :], lambda kf: r.wkv_ref.at[full_half, :HS])
    wv_f = to_f(lambda kf: r.wv_in.at[mine_half, :], lambda kf: r.wkv_ref.at[full_half, HS:])
    wq_f = to_f(lambda kf: r.wq_in.at[mine_half, :], lambda kf: r.wq_ref.at[full_half, :])
    wo_f = to_f(lambda kf: r.wo_in.at[mine_half, :], lambda kf: r.wo_ref.at[full_half, :])
    up_f = to_f(
        lambda kf: r.up_in.at[:, span((lax.rem(f + kf, F) * 2 + c) * shard, shard)], lambda kf: r.up_ref.at[mine, :]
    )
    cot_f = to_f(lambda kf: r.cot_in, lambda kf: r.cot_all.at[kf, :tok])
    cot_c = [start(r.cot_in, r.cot_all.at[0, tok:], sibling)]

    local = [
        pltpu.make_async_copy(src, dst, r.loc_sem.at[i])
        for i, (src, dst) in enumerate(
            (
                (r.wq_in, r.wq_ref.at[mine, :]),
                (r.wo_in, r.wo_ref.at[mine, :]),
                (r.up_in.at[:, span((f * 2 + c) * shard, shard)], r.up_ref.at[mine, :]),
                (r.cot_in, r.cot_all.at[0, :tok]),
                (r.down_in.at[span(c * shard, shard), :], r.down_ref),
            )
        )
    ]
    for copy in local:
        copy.start()

    def weight_halves(copies, ref, cols):
        passed = []
        for kf in range(1, F):
            copies[kf - 1].wait_recv()
            rows = span((lower("f", kf) * 2 + c) * half, half)
            passed.append(start(ref.at[rows, cols], ref.at[rows, cols], sibling))
        return passed

    n_rows = 64

    def unit_rows(i, carry):
        rows = span(i * n_rows, n_rows)
        stream = r.tokens[rows, :].astype(F32)
        inverse = lax.rsqrt(jnp.mean(stream * stream, axis=1, keepdims=True) + EPS)
        r.inv_ref[rows, :] = inverse
        return carry

    lax.fori_loop(0, tok // n_rows, unit_rows, 0)
    r.wkv_ref[mine, :HS] = r.wk_in[...]
    r.wkv_ref[mine, HS:] = r.wv_in[...]
    r.gains_all[f] = r.gains_in[...]
    for copy in gains_f:
        copy.wait_recv()
    for i in range(F):
        both = r.gains_all[i].astype(F32)
        cols = slice(i * own_rows, (i + 1) * own_rows)
        r.gain_ref[0:1, cols] = both[0:1, :]
        r.gain2_ref[0:1, cols] = both[1:2, :]

    def normed_rows(i, carry):
        rows = span(i * n_rows, n_rows)
        r.n1_ref[rows, :] = (r.tokens[rows, :].astype(F32) * r.inv_ref[rows, :] * r.gain_ref[...]).astype(BF)
        return carry

    lax.fori_loop(0, tok // n_rows, normed_rows, 0)

    wkv_c = weight_halves(wk_f, r.wkv_ref, slice(0, HS)) + weight_halves(wv_f, r.wkv_ref, slice(HS, 2 * HS))
    for copy in wkv_c:
        copy.wait_recv()
    kv = r.kv_ref

    def block(a_, b_, c_):
        return kv.at[span(((a_ * B + b_) * 2 + c_) * tok, tok), :]

    kv[span(s * tok, tok), :] = nn(r.n1_ref[...], r.wkv_ref[...]).astype(BF)
    kv_z, kv_x, kv_c = slots(A - 1), slots((B - 1) * A), slots(B * A)
    own = block(a, b, c)
    z_copies = [remote(own, own, kv_z + k - 1, device("a", k)) for k in range(1, A)]

    def guarded(k, ok, act):
        if k == 0:
            act()
        else:
            pl.when(ok)(act)

    for k in range(1, A):
        guarded(k, a + k < A, z_copies[k - 1].start)

    def x_copy(kb, k):
        here = block(jnp.maximum(a - k, 0), b, c)
        return remote(here, here, kv_x + (kb - 1) * A + k, device("b", kb))

    def c_copy(kb, k):
        here = block(jnp.maximum(a - k, 0), lower("b", kb) if kb else b, c)
        return remote(here, here, kv_c + kb * A + k, sibling)

    def pass_on(k):
        for kb in range(1, B):
            x_copy(kb, k).start()
        c_copy(0, k).start()

    pass_on(0)

    local[0].wait()
    wq_c = weight_halves(wq_f, r.wq_ref, slice(0, D))
    for copy in wq_c:
        copy.wait_recv()
    n_cols = 256

    def columns(n, act):
        def body(i, carry):
            act(span(i * n_cols, n_cols))
            return carry

        lax.fori_loop(0, n // n_cols, body, 0)

    def query_cols(cols):
        r.q_ref[:, cols] = nn(r.n1_ref[...], r.wq_ref[:, cols]).astype(BF)

    columns(D, query_cols)

    for k in range(1, A):

        def arrived(k=k):
            z_copies[k - 1].wait_recv()
            pass_on(k)

        guarded(k, a - k >= 0, arrived)

    factor = math.log2(math.e) / math.sqrt(HS)
    r.top[...] = jnp.full(r.top.shape, -3e38, F32)
    r.total[...] = jnp.zeros(r.total.shape, F32)
    r.acc[...] = jnp.zeros(r.acc.shape, F32)
    pos = s * tok + lax.broadcasted_iota(jnp.int32, (1, tok), 1)
    begin = jnp.zeros((1, tok), jnp.int32)
    for i in range(r.ends.shape[0]):
        begin = jnp.maximum(begin, jnp.where(r.ends[i] <= pos, r.ends[i], 0))

    def step(j, masked):
        rows = span(j * CHUNK, CHUNK)
        keys = kv[rows, :HS]
        values_t = kv[rows, HS:].T
        if masked:
            at = j * CHUNK + lax.broadcasted_iota(jnp.int32, (CHUNK, tok), 0)
            mask = jnp.logical_and(at >= begin, at <= pos)
        for h in range(H):
            scores = nt(keys, r.q_ref[:, h * HS : (h + 1) * HS])
            if masked:
                scores = jnp.where(mask, scores, NEG)
            old = r.top[h : h + 1, :]
            new = jnp.maximum(old, jnp.max(scores, axis=0, keepdims=True) * factor)
            shrink = jnp.exp2(old - new)
            probs = jnp.exp2(scores * factor - new)
            r.total[h : h + 1, :] = r.total[h : h + 1, :] * shrink + jnp.sum(probs, axis=0, keepdims=True)
            r.acc[h] = r.acc[h] * shrink + nn(values_t, probs.astype(BF))
            r.top[h : h + 1, :] = new

    last = s // 2
    c_copy(0, 0).wait_recv()
    step(last, True)
    for kb in range(1, B):
        for k in range(A):

            def arrived(kb=kb, k=k):
                x_copy(kb, k).wait_recv()
                c_copy(kb, k).start()

            guarded(k, a - k >= 0, arrived)
    for kb in range(B):
        for k in range(A):
            if kb or k:
                guarded(k, a - k >= 0, c_copy(kb, k).wait_recv)

    def attention_chunk(j, carry):
        plain = jnp.logical_and(j > 0, s < 2 * A * B - 1)

        @pl.when(plain)
        def _():
            step(j, False)

        @pl.when(jnp.logical_not(plain))
        def _():
            step(j, True)

        return carry

    lax.fori_loop(0, last, attention_chunk, 0)
    for h in range(H):
        mixed = r.acc[h] * (1.0 / r.total[h : h + 1, :])
        r.att_ref[:, h * HS : (h + 1) * HS] = mixed.T.astype(BF)
    r.lse_ref[...] = r.top[...] + jnp.log2(r.total[...])

    local[1].wait()
    wo_c = weight_halves(wo_f, r.wo_ref, slice(0, D))
    for copy in wo_c:
        copy.wait_recv()
    squares = jnp.zeros((tok, 1), F32)
    for i in range(D // n_cols):
        cols = slice(i * n_cols, (i + 1) * n_cols)
        part = r.tokens[:, cols].astype(F32) + nn(r.att_ref[...], r.wo_ref[:, cols])
        r.res_ref[:, cols] = part
        squares = squares + jnp.sum(part * part, axis=1, keepdims=True)
    r.inv2_ref[...] = lax.rsqrt(squares * (1.0 / D) + EPS)

    def second_norm(i, carry):
        rows = span(i * n_rows, n_rows)
        r.n2_all[0, rows, :] = (r.res_ref[rows, :] * r.inv2_ref[rows, :] * r.gain2_ref[...]).astype(BF)
        return carry

    lax.fori_loop(0, tok // n_rows, second_norm, 0)

    n2_f = to_f(lambda kf: r.n2_all.at[0, :tok], lambda kf: r.n2_all.at[kf, :tok])
    n2_c = [start(r.n2_all.at[0, :tok], r.n2_all.at[0, tok:], sibling)]
    local[2].wait()
    local[3].wait()
    local[4].wait()
    for copy in up_f:
        copy.wait_recv()
    for kf in range(1, F):
        cot_f[kf - 1].wait_recv()
        cot_c.append(start(r.cot_all.at[kf, :tok], r.cot_all.at[kf, tok:], sibling))

    def feed_forward(kf):
        def hidden_cols(cols):
            before = nn(r.n2_all[kf], r.up_ref[:, cols])
            d_hidden = nt(r.cot_all[kf], r.down_ref[cols, :])
            sig = 1.0 / (1.0 + jnp.exp(-before))
            r.hid_all[kf, :, cols] = (before * sig).astype(BF)
            r.dp_all[kf, :, cols] = (d_hidden * sig * (1.0 + before * (1.0 - sig))).astype(BF)

        columns(shard, hidden_cols)

        def back_cols(cols):
            r.back_s[kf, :, cols] = nt(r.dp_all[kf], r.up_ref[cols, :]).astype(BF)

        columns(D, back_cols)
        return start(r.back_s.at[kf, tok:], r.back_c.at[kf], sibling)

    def out_part(kf):
        def out_cols(cols):
            r.out_s[kf, :, cols] = nn(r.hid_all[kf], r.down_ref[:, cols]).astype(BF)

        columns(D, out_cols)
        return start(r.out_s.at[kf, tok:], r.out_c.at[kf], sibling)

    def chip_sum(kf, part, other, ref):
        def rows_sum(i, carry):
            rows = span(i * n_rows, n_rows)
            ref[kf - 1, rows, :] = (part[kf, rows, :].astype(F32) + other[kf, rows, :].astype(F32)).astype(BF)
            return carry

        lax.fori_loop(0, tok // n_rows, rows_sum, 0)

    back_copies, out_copies, back_back, out_back = [None] * F, [None] * F, [], []
    n2_c[0].wait_recv()
    cot_c[0].wait_recv()
    back_copies[0] = feed_forward(0)
    for kf in range(1, F):
        n2_f[kf - 1].wait_recv()
        n2_c.append(start(r.n2_all.at[kf, :tok], r.n2_all.at[kf, tok:], sibling))
    for kf in range(1, F):
        n2_c[kf].wait_recv()
        cot_c[kf].wait_recv()
        back_copies[kf] = feed_forward(kf)
        out_copies[kf] = out_part(kf)
        back_copies[kf].wait_recv()
        chip_sum(kf, r.back_s, r.back_c, r.back_y)
        back_back.append(start(r.back_y.at[kf - 1], r.back_r.at[kf - 1], device("f", F - kf)))

    n_out = 128

    def down_grad(i, carry):
        cols = span(i * n_out, n_out)
        r.gd_ref[cols, :] = sum(tn(r.hid_all[kf, :, cols], r.cot_all[kf]) for kf in range(F)).astype(BF)
        return carry

    lax.fori_loop(0, shard // n_out, down_grad, 0)
    x.send_down(0, 1)

    def up_grad(i, carry):
        cols = span(i * n_out, n_out)
        rows = span(lax.rem(i, own_rows // n_out) * n_out, n_out)
        grad = sum(tn(r.n2_all[kf, :, cols], r.dp_all[kf]) for kf in range(F))
        r.gu_ref[i // (own_rows // n_out), rows, :] = grad.astype(BF)
        return carry

    lax.fori_loop(0, D // n_out, up_grad, 0)
    x.send_up(0, 1)
    for i in range(1, A):
        x.send_down(i, i + 1)
        x.send_up(i, i + 1)
    for kf in range(1, F):
        out_copies[kf].wait_recv()
        chip_sum(kf, r.out_s, r.out_c, r.out_y)
        out_back.append(start(r.out_y.at[kf - 1], r.out_r.at[kf - 1], device("f", F - kf)))
    out_copies[0] = out_part(0)

    back_copies[0].wait_recv()
    for copy in back_back:
        copy.wait_recv()

    def norm_back(i, gain_grad):
        rows = span(i * n_rows, n_rows)
        d_normed = r.back_s[0, rows, :].astype(F32) + r.back_c[0, rows, :].astype(F32)
        for kf in range(1, F):
            d_normed = d_normed + r.back_r[kf - 1, rows, :].astype(F32)
        inverse = r.inv2_ref[rows, :]
        unit = r.res_ref[rows, :] * inverse
        weighted = d_normed * unit
        scaled = d_normed * r.gain2_ref[...]
        mean = jnp.mean(scaled * unit, axis=1, keepdims=True)
        d_residual = r.cot_all[0, rows, :].astype(F32) + inverse * (scaled - unit * mean)
        r.dres_ref[rows, :] = d_residual
        r.dbr_ref[rows, :] = d_residual.astype(BF)
        return gain_grad + jnp.sum(weighted, axis=0, keepdims=True)

    r.gain_rows[1:2, :] = lax.fori_loop(0, tok // n_rows, norm_back, jnp.zeros((1, D), F32))

    def attended_cols(cols):
        r.d_ref[:, cols] = nt(r.dbr_ref[...], r.wo_ref[cols, :]).astype(BF)

    columns(D, attended_cols)

    done(n2_f + n2_c)

    def out_grad(i, carry):
        cols = span(i * n_out, n_out)
        rows = span(lax.rem(i, own_rows // n_out) * n_out, n_out)
        r.go_ref[i // (own_rows // n_out), rows, :] = tn(r.att_ref[:, cols], r.dbr_ref[...]).astype(BF)
        return carry

    lax.fori_loop(0, D // n_out, out_grad, 0)

    def finish_output():
        out_copies[0].wait_recv()
        for copy in out_back:
            copy.wait_recv()

        def output_rows(i, carry):
            rows = span(i * n_rows, n_rows)
            value = r.res_ref[rows, :] + r.out_s[0, rows, :].astype(F32) + r.out_c[0, rows, :].astype(F32)
            for kf in range(1, F):
                value = value + r.out_r[kf - 1, rows, :].astype(F32)
            r.out_ref[rows, :] = value.astype(BF)
            return carry

        lax.fori_loop(0, tok // n_rows, output_rows, 0)
        done(out_copies)
        results[0].start()

    results = [
        pltpu.make_async_copy(src, dst, r.loc_sem.at[5 + i])
        for i, (src, dst) in enumerate(((r.out_ref, r.out_hbm), (r.grad_tokens, r.grad_hbm)))
    ]

    def finish():
        results[1].start()
        for copy in results:
            copy.wait()
        for copy in sent:
            copy.wait_send()
        for k in range(1, A):
            guarded(k, a + k < A, z_copies[k - 1].wait_send)
        for k in range(A):
            for kb in range(B):
                if kb:
                    guarded(k, a - k >= 0, x_copy(kb, k).wait_send)
                guarded(k, a - k >= 0, c_copy(kb, k).wait_send)

    return finish_output, finish


AGAIN = {
    "go_ref": "n2_all",
    "gq_ref": "out_s",
    "dn1": "res_ref",
    "grad_tokens": "res_ref",
    "dq": "d_ref",
    "out_ref": "dbr_ref",
    "tok_ref": "tokens",
}


def layer_shapes(dims, tok, D, shard, window):
    A, B, F = dims
    own_rows = D // F
    outs, scratch = tail_shapes(dims, tok, D, shard, window, 16 * F + A - 1 + (B - 1) * A + B * A)

    def low(*shape):
        return pltpu.VMEM(shape, BF)

    def wide(*shape):
        return pltpu.VMEM(shape, F32)

    pair = [low(F, 2 * tok, D), low(F, tok, D), low(F - 1, tok, D), low(F - 1, tok, D)]
    first = [
        low(tok, D),
        low(window, 2 * HS),
        low(tok, D),
        low(tok, D),
        wide(H, tok),
        low(shard, D),
        low(F, own_rows, shard),
        low(tok, D),
        low(D, D),
        low(D, 2 * HS),
        wide(tok, 1),
        wide(1, D),
        wide(tok, D),
        wide(1, D),
        low(D, D),
        low(D, shard),
        low(shard, D),
        low(F, 16, own_rows),
        low(F, 2 * tok, D),
        low(F, 2 * tok, D),
        low(F, 2 * tok, shard),
        low(F, 2 * tok, shard),
        wide(tok, D),
        wide(tok, 1),
        low(tok, D),
        *pair,
        *pair,
        wide(H, tok),
        wide(H, tok),
        pltpu.SemaphoreType.DMA((7,)),
    ]
    sizes = dict(zip(HEAD_SCRATCH + TAIL_SCRATCH, first + scratch))
    fits = all(sizes[k].shape == sizes[AGAIN[k]].shape for k in ("gq_ref", "dn1", "dq")) and own_rows == 2 * tok
    scratch = [ref for name, ref in zip(TAIL_SCRATCH, scratch) if name not in AGAIN]
    fits = fits and vmem_bytes(first + scratch) + 4 * 2**20 < LIMIT
    return outs + (jax.ShapeDtypeStruct((tok, D), BF),), first + scratch, fits


def vmem_bytes(scratch):
    total = 0
    for ref in scratch:
        shape = getattr(ref, "shape", ())
        if len(shape) >= 2:
            lanes = -(-shape[-1] // 128) * 128
            rows = -(-shape[-2] // 8) * 8
            total += math.prod(shape[:-2]) * rows * lanes * jnp.dtype(ref.dtype).itemsize
    return total


def layer(dims, ends, tokens, gains, w_key, w_value, cotangent, w_query, w_out, w_up, w_down, outs, scratch):
    tok, D = tokens.shape
    hbm = pl.BlockSpec(memory_space=pltpu.HBM)
    names = HEAD_IN + TAIL_OUT[:5] + ("grad_hbm", "out_hbm") + HEAD_SCRATCH + tuple(n for n in TAIL_SCRATCH if n not in AGAIN)
    return pl.pallas_call(
        functools.partial(tail_kernel, dims, head, names),
        out_shape=outs,
        in_specs=[SMEM] + [VMEM] * 4 + [hbm] * 5,
        out_specs=(hbm,) * 7,
        scratch_shapes=scratch,
        compiler_params=pltpu.CompilerParams(vmem_limit_bytes=LIMIT, collective_id=2, has_side_effects=True),
        cost_estimate=pl.CostEstimate(flops=2**35, bytes_accessed=2**25, transcendentals=2**24),
        name="layer",
    )(ends, tokens, gains, w_key, w_value, cotangent, w_query, w_out, w_up, w_down)


def after(value, *others):
    return lax.optimization_barrier((value, *others))[0]


class Grid:
    def __init__(self):
        seq = lax.axis_size("seq")
        self.F = lax.axis_size("fsdp")
        self.C = 2
        chips = seq // 2
        self.B = 2 if chips == 8 else chips // 2
        self.A = chips // self.B
        self.s = lax.axis_index("seq")
        self.f = lax.axis_index("fsdp")
        self.c = self.s % 2
        self.b = self.s // 2 % self.B
        self.a = self.s // (2 * self.B)

    def size(self, axis):
        return {"a": self.A, "b": self.B, "c": self.C, "f": self.F}[axis]

    def place(self, axis):
        return {"a": self.a, "b": self.b, "c": self.c, "f": self.f}[axis]

    def send(self, value, axis, step, upward=False):
        pairs = []
        for a in range(self.A):
            for b in range(self.B):
                for c in range(2):
                    for f in range(self.F):
                        at = {"a": a, "b": b, "c": c, "f": f}
                        to = dict(at)
                        to[axis] += step
                        if upward and not 0 <= to[axis] < self.size(axis):
                            continue
                        to[axis] %= self.size(axis)
                        line = [((d["a"] * self.B + d["b"]) * 2 + d["c"]) * self.F + d["f"] for d in (at, to)]
                        pairs.append(tuple(line))
        return lax.ppermute(value, ("seq", "fsdp"), pairs)

    def stack(self, parts, axis):
        n, me = len(parts), self.place(axis)
        if n == 2:
            low = me == 0
            return jnp.stack([jnp.where(low, parts[0], parts[1]), jnp.where(low, parts[1], parts[0])])
        twice = jnp.stack(parts + parts)
        return lax.dynamic_slice_in_dim(twice, (n - me) % n, n, 0)

    def gather(self, value, axis):
        n = self.size(axis)
        return self.stack([value] + [self.send(value, axis, -k) for k in range(1, n)], axis)

    def scatter(self, parts, axis):
        n, me = self.size(axis), self.place(axis)

        def pick(k):
            return lax.dynamic_index_in_dim(parts, (me + k) % n, 0, keepdims=False)

        got = [self.send(pick(k).astype(BF), axis, k) for k in range(1, n)]
        total = pick(0).astype(F32)
        for piece in got:
            total = total + piece.astype(F32)
        return total

    def plane_sum(self, parts):
        half = self.scatter(parts, "b").astype(BF)
        return self.scatter(half, "a")

    def plane_gather(self, share):
        rows = self.gather(share.astype(BF), "a")
        return self.gather(rows, "b")


def local(
    tokens,
    cotangent,
    seq_lengths,
    group_of_shard,
    gain_attn,
    w_query,
    w_key,
    w_value,
    w_out,
    gain_ffn,
    w_up,
    w_down,
):
    g = Grid()
    A, B, C, F = g.A, g.B, g.C, g.F
    tok, D = tokens.shape[1:]
    FF = w_up.shape[1]
    own_rows = D // F
    seq_parts = A * B * C
    shard = FF // (2 * F)

    group = lax.dynamic_index_in_dim(group_of_shard, g.f, 0, keepdims=False)
    lengths = lax.dynamic_index_in_dim(seq_lengths, group, 0, keepdims=False)
    running, ends = jnp.int32(0), []
    for i in range(seq_lengths.shape[1]):
        running = running + lengths[i]
        ends.append(running)
    scal = jnp.stack([g.s.astype(jnp.int32), *ends])

    outs, scratch, fits = layer_shapes((A, B, F), tok, D, shard, seq_parts * tok)
    if fits:
        gains = jnp.pad(jnp.stack([gain_attn, gain_ffn]), ((0, 14), (0, 0)))
        *grads, grad_tokens, output = layer(
            (A, B, F), scal[1:], tokens[0], gains, w_key, w_value, cotangent[0], w_query, w_out, w_up, w_down, outs, scratch
        )
        return results(output, grad_tokens, *grads)

    gains = jnp.stack([gain_attn, gain_ffn])
    full_gains = g.gather(gains, "f").transpose(1, 0, 2).reshape(2, D).astype(F32)
    gain_first, gain_second = full_gains[0], full_gains[1]
    own_kv = jnp.concatenate([w_key, w_value], axis=1)
    full_kv = g.gather(own_kv, "f").reshape(D, 2 * HS)

    def gather_weight(weight, *late):
        half = own_rows // 2
        mine = lax.dynamic_slice_in_dim(weight, g.c * half, half, 0)
        if late:
            mine = after(mine, *late)
        pieces = [g.gather(g.send(mine, "f", -k), "c").reshape(weight.shape) for k in range(1, F)]
        return g.stack([weight] + pieces, "f").reshape(F * own_rows, -1)

    full_query = gather_weight(w_query)

    stream = tokens[0].astype(F32)
    inverse_first = lax.rsqrt(jnp.mean(stream * stream, axis=1, keepdims=True) + EPS)
    unit_first = stream * inverse_first
    normed_first = (unit_first * gain_first).astype(BF)
    key_value = nn(normed_first, full_kv).astype(BF)
    queries = nn(normed_first, full_query).astype(BF)

    column = [key_value] + [g.send(key_value, "a", k, upward=True) for k in range(1, A)]
    twice = jnp.stack(column[::-1] + column[::-1])
    column = lax.dynamic_slice_in_dim(twice, A - 1 - g.a, A, 0)
    plane = g.gather(column, "b")
    whole = g.gather(plane, "c")
    window_kv = whole.transpose(2, 1, 0, 3, 4).reshape(seq_parts * tok, 2 * HS)

    full_out = gather_weight(w_out, full_query)
    upstream = cotangent[0]
    cot = []
    for k in range(F):
        mine = upstream if k == 0 else g.send(after(upstream, full_query), "f", k)
        cot.append(jnp.concatenate([mine, g.send(mine, "c", 1)], axis=0))
    ups = w_up.reshape(own_rows, F, 2, shard)
    up_parts = []
    for k in range(F):
        block = lax.dynamic_slice(ups, (0, (g.f + k) % F, g.c, 0), (own_rows, 1, 1, shard)).reshape(own_rows, shard)
        up_parts.append(block if k == 0 else g.send(after(block, full_out), "f", k))
    up_parts = [up_parts[0]] + up_parts[1:][::-1]
    up = g.stack(up_parts, "f").reshape(D, shard)
    down = lax.dynamic_slice_in_dim(w_down, g.c * shard, shard, 0)

    attended, lse = attend(scal, queries, window_kv)

    residual = stream + nn(attended, full_out)
    inverse_second = lax.rsqrt(jnp.mean(residual * residual, axis=1, keepdims=True) + EPS)
    unit_second = residual * inverse_second
    normed_second = (unit_second * gain_second).astype(BF)

    out_sum, back_sum = residual, jnp.zeros((tok, D), F32)
    hiddens, d_pres, norms = [], [], []
    backs, outs = [], []
    for k in range(F):
        mine = normed_second if k == 0 else g.send(normed_second, "f", k)
        norm = jnp.concatenate([mine, g.send(mine, "c", 1)], axis=0)
        before = nn(norm, up)
        d_hidden = nt(cot[k], down)
        sig = jax.nn.sigmoid(before)
        hidden = (before * sig).astype(BF)
        d_pre = (d_hidden * sig * (1.0 + before * (1.0 - sig))).astype(BF)
        back = nt(d_pre, up)
        out = nn(hidden, down)
        hiddens.append(hidden)
        d_pres.append(d_pre)
        norms.append(norm)
        backs.append(back)
        outs.append(out)

    def give_back(parts):
        total = 0.0
        for k, part in enumerate(parts):
            other = g.send(part[tok:].astype(BF), "c", 1)
            chip = part[:tok] + other.astype(F32)
            if k:
                chip = g.send(chip.astype(BF), "f", -k).astype(F32)
            total = total + chip
        return total

    d_normed_second = give_back(backs)
    output = (residual + give_back(outs)).astype(BF)

    grad_down = sum(tn(h, c) for h, c in zip(hiddens, cot)).astype(BF)
    grad_up = sum(tn(n, d) for n, d in zip(norms, d_pres)).astype(BF)

    def norm_back(gradient, unit_rows, inverse, gain_vec):
        scaled = gradient * gain_vec
        gain_grad = jnp.sum(gradient * unit_rows, axis=0)
        return gain_grad, inverse * (scaled - unit_rows * jnp.mean(scaled * unit_rows, axis=1, keepdims=True))

    gain_second_grad, d_from_norm = norm_back(d_normed_second, unit_second, inverse_second, gain_second)
    d_residual = upstream.astype(F32) + d_from_norm
    d_branch = d_residual.astype(BF)
    d_attended = nt(d_branch, full_out).astype(BF)
    grad_out = tn(attended, d_branch).astype(BF)

    down_all, up_all, out_all, query_all, kv_all, grad_tokens = tail(
        (A, B, F),
        scal[1:],
        queries,
        window_kv,
        d_attended,
        attended,
        lse,
        grad_down,
        grad_up.reshape(F, own_rows, shard),
        grad_out.reshape(F, own_rows, D),
        normed_first,
        full_query,
        full_kv,
        tokens[0],
        inverse_first,
        gain_first[None],
        d_residual,
        gain_second_grad[None],
    )
    return results(output, grad_tokens, down_all, up_all, out_all, query_all, kv_all)


def results(output, grad_tokens, down_all, up_all, out_all, query_all, kv_all):
    F, own_rows = up_all.shape[:2]
    grad_w_up = jnp.concatenate([up_all[i].astype(F32) for i in range(F)], axis=1)
    r_kv = own_rows // kv_all.shape[1]
    grad_kv = kv_all[:, :, :r_kv].astype(F32).reshape(2, own_rows, HS)
    gain_grads = kv_all[:, 0, r_kv : r_kv + own_rows // 128].astype(F32).reshape(2, own_rows)
    return (
        output[None],
        grad_tokens[None],
        gain_grads[0],
        query_all.astype(F32),
        grad_kv[0],
        grad_kv[1],
        out_all.astype(F32),
        gain_grads[1],
        grad_w_up,
        down_all.astype(F32),
    )


def solution(mesh):
    placed = (
        P("fsdp", "seq", None),
        P("fsdp", "seq", None),
        P(),
        P(),
        P("fsdp"),
        P("fsdp", None),
        P("fsdp", None),
        P("fsdp", None),
        P("fsdp", None),
        P("fsdp"),
        P("fsdp", None),
        P("fsdp", None),
    )
    return jax.shard_map(
        local,
        mesh=mesh,
        in_specs=placed,
        out_specs=(
            P("fsdp", "seq", None),
            P("fsdp", "seq", None),
            P("fsdp"),
            P("fsdp", None),
            P("fsdp", None),
            P("fsdp", None),
            P("fsdp", None),
            P("fsdp"),
            P("fsdp", None),
            P("fsdp", None),
        ),
        check_vma=False,
    )
```

profile of v0, /device:TPU:0, one launch (start us, length us, event | category | flops | bytes accessed | tf_op | source)
XLA Modules:
  0.0 292.4 jit_solution(1881812143442284950)
XLA Ops:
  0.6 0.0 copy-start
  0.7 1.2 dynamic_slice.8
  3.8 0.0 copy-done
  3.9 0.6 fusion.4
  6.4 1.2 pad_add_fusion.refs_0_
  7.6 0.7 stack.21
  8.3 0.7 stack.22
  9.0 0.6 fusion.2.refs_2_
  9.6 264.6 %layer.1 = (bf16[2048,1024]{1,0:T(8,128)(2,1)}, bf16[2,512,2048]{2,1,0:T(8,128)(2,1)}, bf16[512,1024]{1,0:T(8,128)(2,1)}, bf16[512,1024]{1,0:T(8,128)(2,1)}, bf1...) custom-call(s32[3]{0:T(128)} %pad_add_fusion.refs_0_, bf16[256,1024]{1,0:T(8,128)(2,1)} %bitcast.22, ...), custom_call_target="tpu_custom_call" | custom-call | flops 34359738368 | bytes 33554432 | tf_op jit(solution)/shard_map/layer/pallas_call | solution.py:1357
  274.3 2.8 slice_bitcast_fusion.1
  277.1 0.0 copy-start.1
  277.1 4.5 %maximum_convert_fusion = f32[512,4096]{1,0:T(8,128)} fusion(bf16[512,2048]{1,0:T(8,128)(2,1)S(1)} %get-tuple-element.25, bf16[512,2048]{1,0:T(8,128)(2,1)S(1)} %get-tuple-element.24), kind=kLoop, calls=%fused_computation | loop fusion | flops 8388608 | bytes 12582912 | tf_op jit(solution)/shard_map/concatenate | solution.py:1603
  281.6 0.0 copy-done.1
  281.6 0.0 copy-start.3
  281.6 0.0 copy-start.2
  281.6 4.5 %convert_element_type.32 = f32[2048,1024]{1,0:T(8,128)} convert(bf16[2048,1024]{1,0:T(8,128)(2,1)S(1)} %copy-done.1) | non-fusion elementwise | flops 2097152 | bytes 12582912 | tf_op jit(solution)/shard_map/convert_element_type | solution.py:1617
  286.0 0.0 copy-start.6
  286.0 0.0 copy-start.5
  286.0 0.0 copy-done.3
  286.0 0.0 copy-start.4
  286.0 1.6 convert_element_type.27
  287.6 0.0 copy-done.2
  287.6 1.6 convert_element_type.29
  289.2 0.0 copy-done.6
  289.2 0.8 fusion.3
  290.1 0.6 slice_bitcast_fusion.2
  290.6 0.0 copy-done.5
  290.6 0.8 copy.24
  291.4 0.0 copy-done.4
  291.4 1.0 copy.25
  (3 shorter events, 0.0 us)
Async XLA Ops:
  0.6 3.2 %copy-start = (s32[2,3]{1,0:T(2,128)S(1)}, s32[2,3]{1,0:T(2,128)}, u32[]{:S(2)}) copy-start(s32[2,3]{1,0:T(2,128)} %param.14) | copy-start | bytes 76
  277.1 4.5 %copy-start.1 = (bf16[2048,1024]{1,0:T(8,128)(2,1)S(1)}, bf16[2048,1024]{1,0:T(8,128)(2,1)}, u32[]{:S(2)}) copy-start(bf16[2048,1024]{1,0:T(8,128)(2,1)} %get-tuple-element.23) | copy-start | bytes 12582916
  281.6 4.5 %copy-start.3 = (bf16[512,1024]{1,0:T(8,128)(2,1)S(1)}, bf16[512,1024]{1,0:T(8,128)(2,1)}, u32[]{:S(2)}) copy-start(bf16[512,1024]{1,0:T(8,128)(2,1)} %get-tuple-element.20) | copy-start | bytes 3145732
  281.6 6.1 %copy-start.2 = (bf16[512,1024]{1,0:T(8,128)(2,1)S(1)}, bf16[512,1024]{1,0:T(8,128)(2,1)}, u32[]{:S(2)}) copy-start(bf16[512,1024]{1,0:T(8,128)(2,1)} %get-tuple-element.21) | copy-start | bytes 3145732
  286.0 3.1 %copy-start.6 = (bf16[2,4,144,128]{3,2,1,0:T(8,128)(2,1)S(1)}, bf16[2,4,144,128]{3,2,1,0:T(8,128)(2,1)}, u32[]{:S(2)}) copy-start(bf16[2,4,144,128]{3,2,1,0:T(8,128)(2,1)} %get-tuple-element.19) | copy-start | bytes 884740
  286.0 4.6 %copy-start.5 = (bf16[256,1024]{1,0:T(8,128)(2,1)S(1)}, bf16[256,1024]{1,0:T(8,128)(2,1)}, u32[]{:S(2)}) copy-start(bf16[256,1024]{1,0:T(8,128)(2,1)} %get-tuple-element.17) | copy-start | bytes 1572868
  286.0 5.4 %copy-start.4 = (f32[256,1024]{1,0:T(8,128)S(1)}, f32[256,1024]{1,0:T(8,128)}, u32[]{:S(2)}) copy-start(f32[256,1024]{1,0:T(8,128)} %get-tuple-element.18) | copy-start | bytes 3145732
where the time goes:
time: 293 us; the launch traced here: 292 us
  Pallas kernels  265 us (90%)
  other arithmetic  14 us (5%)
  local copies, waits for them, and re-layouts  9.21 us (3%)
  between operations  4.6 us (2%)
    pallas_call x1, Pallas kernels, layer(): pl.pallas_call(functools.partial(tail_kernel, dims, head, names), out_sha...  265 us

commit v1 on v0

--- a/solution.py
+++ b/solution.py
@@ -196,6 +196,10 @@
     "recv_sem",
     "copy_sem",
 )
+
+
+def head_block(h, tok):
+    return slice(h % 2 * HS, (h % 2 + 1) * HS), slice(h // 2 * tok, (h // 2 + 1) * tok)
 
 
 def tail_kernel(dims, head, names, *refs):
@@ -285,6 +289,27 @@
     def lower(axis, step):
         return lax.rem({"a": a + A, "b": b + B, "f": f + F}[axis] - step, {"a": A, "b": B, "f": F}[axis])
 
+    def flip(axis_bit, place=None):
+        place = a if place is None else place
+        return place + axis_bit - 2 * axis_bit * lax.rem(place // axis_bit, 2) if axis_bit else place
+
+    def offset(o):
+        place = a
+        for bit in bits:
+            if o // bit % 2:
+                place = flip(bit, place)
+        return place
+
+    def along_a(bit):
+        return ((flip(bit) * B + b) * 2 + c, f)
+
+    bits = [2**i for i in range(A.bit_length() - 1)]
+    assert 2 ** len(bits) == A
+    order = [o for bit in bits for o in range(A) if o // bit % 2 and o % bit == 0] + [0]
+
+    def low_bit(o):
+        return next((bit for bit in bits if o // bit % 2), A)
+
     used = [0]
 
     def slots(n=1):
@@ -320,7 +345,7 @@
     z_u = slots(A - 1)
 
     def down_copies(i):
-        at = lax.rem(a + 1 + i, A)
+        at = offset(order[i])
         copies = []
         for kb in range(B - 1):
             other = lax.rem(b + kb + 1, B)
@@ -329,7 +354,7 @@
         return copies
 
     def up_copies(i):
-        at = lax.rem(a + 1 + i, A)
+        at = offset(order[i])
         copies = []
         for kb in range(B - 1):
             rows = pl.ds(pl.multiple_of(lax.rem(b + kb + 1, B) * r_u, r_u), r_u)
@@ -347,34 +372,179 @@
             for copy in up_copies(i):
                 copy.start()
 
-    def own_sums(i):
-        at = lax.rem(a + 1 + i, A)
+    def down_sum(i):
+        for copy in down_copies(i):
+            copy.wait()
+        at = offset(order[i])
         rows = pl.ds(pl.multiple_of((b * A + at) * r_d, r_d), r_d)
-        total_d = gd_ref[rows, :].astype(F32)
+        total = gd_ref[rows, :].astype(F32)
+        for kb in range(B - 1):
+            total = total + xr_d[kb, i].astype(F32)
+        return total
+
+    def up_sum(i):
+        for copy in up_copies(i):
+            copy.wait()
+        at = offset(order[i])
         rows = pl.ds(pl.multiple_of(b * r_u, r_u), r_u)
         cols = pl.ds(pl.multiple_of(at * w_u, w_u), w_u)
-        total_u = gu_ref[:, rows, cols].astype(F32)
+        total = gu_ref[:, rows, cols].astype(F32)
         for kb in range(B - 1):
-            total_d = total_d + xr_d[kb, i].astype(F32)
-            total_u = total_u + xr_u[kb, i].astype(F32)
-        return total_d, total_u
+            total = total + xr_u[kb, i].astype(F32)
+        return total
+
+    def z_index(o, bit):
+        return order.index(o + bit)
+
+    def down_z(i):
+        return remote(zs_d.at[i], zr_d.at[i], z_d + i, along_a(low_bit(order[i])))
+
+    def up_z(i):
+        return remote(zs_u.at[i], zr_u.at[i], z_u + i, along_a(low_bit(order[i])))
+
+    def z_added(i, total, copy, got):
+        o = order[i]
+        for bit in bits:
+            if bit < low_bit(o):
+                k = z_index(o, bit)
+                copy(k).wait()
+                total = total + got[k].astype(F32)
+        return total
+
+    def down_step(i):
+        zs_d[i] = z_added(i, down_sum(i), down_z, zr_d).astype(BF)
+        down_z(i).start()
+
+    def up_step(i):
+        zs_u[i] = z_added(i, up_sum(i), up_z, zr_u).astype(BF)
+        up_z(i).start()
+
+    def down_share():
+        sh_d[...] = z_added(A - 1, down_sum(A - 1), down_z, zr_d).astype(BF)
+        gather_down.begin()
+
+    up_y = slots(F - 1)
+
+    def up_y_copy(kf):
+        return remote(yr_u.at[lax.rem(f + kf + 1, F)], sh_u.at[f], up_y + kf, device("f", kf + 1))
+
+    def up_share():
+        total = z_added(A - 1, up_sum(A - 1), up_z, zr_u)
+        yr_u[...] = total.astype(BF)
+        for kf in range(F - 1):
+            up_y_copy(kf).start()
+        sh_u[f] = yr_u[f]
+
+    def up_gather():
+        for kf in range(F - 1):
+            up_y_copy(kf).wait()
+        gather_up.begin()
+
+    gathers = []
+
+    class Gather:
+        def __init__(self, share, view, planes=True):
+            self.share, self.view, self.n = share, view, B if planes else 1
+            self.z_slot = slots(A)
+            self.x_slot = slots((self.n - 1) * A)
+            self.c_slot = slots(self.n * A)
+            self.place = len(gathers)
+            gathers.append(self)
+
+        def local(self):
+            return pltpu.make_async_copy(self.share, self.view(c, b, a), copy_sem.at[self.place])
+
+        def at(self, o, kb=0):
+            return self.view(c, lower("b", kb) if kb else b, offset(o))
+
+        def z(self, bit, o):
+            here = self.at(o)
+            return remote(here if o else self.share, here, self.z_slot + A - A // bit + o // (2 * bit), along_a(bit))
+
+        def x(self, kb, o):
+            here = self.at(o)
+            return remote(here if o else self.share, here, self.x_slot + kb * A + o, device("b", kb + 1))
+
+        def c(self, kb, o):
+            here = self.at(o, kb)
+            return remote(here if kb or o else self.share, here, self.c_slot + kb * A + o, device("c", 1))
+
+        def begin(self):
+            self.local().start()
+            for bit in bits[::-1]:
+                self.z(bit, 0).start()
+            self.pass_on(0)
+
+        def pass_on(self, o):
+            for kb in range(self.n - 1):
+                self.x(kb, o).start()
+            self.c(0, o).start()
+
+        def from_a(self, stages=None):
+            for i, bit in enumerate(bits[::-1]):
+                if stages is not None and i not in stages:
+                    continue
+                for o in range(0, A, 2 * bit):
+                    self.z(bit, o).wait_recv()
+                    for lower_bit in bits[: len(bits) - 1 - i][::-1]:
+                        self.z(lower_bit, o + bit).start()
+                    self.pass_on(o + bit)
+
+        def from_b(self):
+            for kb in range(self.n - 1):
+                for o in self.offsets():
+                    self.x(kb, o).wait_recv()
+                    self.c(kb + 1, o).start()
+
+        def offsets(self):
+            found = [0]
+            for bit in bits[::-1]:
+                found += [o + bit for o in found]
+            return found
+
+        def end(self):
+            self.local().wait()
+            for bit in bits:
+                for o in range(0, A, 2 * bit):
+                    self.z(bit, o).wait_send()
+            for o in range(A):
+                for kb in range(self.n - 1):
+                    self.x(kb, o).wait_send()
+                for kb in range(self.n):
+                    self.c(kb, o).wait()
+
+    def view_down(c_, b_, a_):
+        return out_down.at[pl.ds(pl.multiple_of(((c_ * B + b_) * A + a_) * r_d, r_d), r_d), :]
+
+    def view_up(c_, b_, a_):
+        rows = pl.ds(pl.multiple_of(b_ * r_u, r_u), r_u)
+        return out_up.at[:, rows, pl.ds(pl.multiple_of(c_ * shard + a_ * w_u, w_u), w_u)]
+
+    half = D // 2
+    w_o = half // A
+
+    def view_square(out):
+        def view(c_, b_, a_):
+            rows = pl.ds(pl.multiple_of(b_ * r_u, r_u), r_u)
+            return out.at[rows, pl.ds(pl.multiple_of(c_ * half + a_ * w_o, w_o), w_o)]
+
+        return view
+
+    gather_down = Gather(sh_d, view_down)
+    gather_up = Gather(sh_u, view_up)
+    gather_o = Gather(o_s, view_square(out_o))
+    gather_q = Gather(q_s, view_square(out_q))
+    gather_kv = Gather(kv_s, lambda c_, b_, a_: out_kv.at[c_, a_], planes=False)
 
     if head is None:
-        for i in range(A):
-            send_down(i, i + 1)
-            send_up(i, i + 1)
+        send_down(0, A)
+        send_up(0, A)
     else:
         own = types.SimpleNamespace(
             A=A, B=B, F=F, a=a, b=b, c=c, f=f, s=s, slots=slots, remote=remote, device=device, lower=lower,
-            send_down=send_down, send_up=send_up,
+            send_down=send_down, send_up=send_up, down_step=down_step,
         )
         finish_output, finish_head = head(r, own)
-
-    half = D // 2
-
-    def reduce_c(ref, got, width):
-        other = pl.ds(pl.multiple_of((1 - c) * width, width), width)
-        return start(ref.at[:, :, other], got, slots(), device("c", 1))
 
     def reduce_y(ref, got, sent, width):
         mine = pl.ds(pl.multiple_of(c * width, width), width)
@@ -385,7 +555,66 @@
 
         lax.fori_loop(0, F, add, 0)
 
-    o_c_copy = reduce_c(go_ref, o_c, half)
+    class Square:
+        def __init__(self, grad, got_c, got_y, got_x, got_z, share, gather):
+            self.grad, self.got_c, self.got_y, self.got_x, self.got_z = grad, got_c, got_y, got_x, got_z
+            self.share, self.gather = share, gather
+            self.c_slot, self.y_slot, self.x_slot = slots(), slots(F - 1), slots(B - 1)
+
+        def c(self):
+            other = pl.ds(pl.multiple_of((1 - c) * half, half), half)
+            return remote(self.grad.at[:, :, other], self.got_c, self.c_slot, device("c", 1))
+
+        def y(self, kf):
+            return remote(self.got_c.at[lax.rem(f + kf + 1, F)], self.got_y.at[kf], self.y_slot + kf, device("f", kf + 1))
+
+        def over_c(self):
+            self.c().start()
+
+        def over_f(self):
+            self.c().wait()
+            reduce_y(self.grad, self.got_c, self.got_c, half)
+            for kf in range(F - 1):
+                self.y(kf).start()
+
+        def over_b(self):
+            total = self.got_c[f].astype(F32)
+            for kf in range(F - 1):
+                self.y(kf).wait()
+                total = total + self.got_y[kf].astype(F32)
+            self.got_y[F - 1] = total.astype(BF)
+            for kb in range(B - 1):
+                self.x(kb).start()
+
+        def x(self, kb):
+            rows = pl.ds(pl.multiple_of(lax.rem(b + kb + 1, B) * r_u, r_u), r_u)
+            return remote(self.got_y.at[F - 1, rows, :], self.got_x.at[kb], self.x_slot + kb, device("b", kb + 1))
+
+        def over_a(self):
+            rows = pl.ds(pl.multiple_of(b * r_u, r_u), r_u)
+            total = self.got_y[F - 1, rows, :].astype(F32)
+            for kb in range(B - 1):
+                self.x(kb).wait()
+                total = total + self.got_x[kb].astype(F32)
+            self.got_x[B - 1] = total.astype(BF)
+            self.copies = []
+            for ka in range(A - 1):
+                cols = pl.ds(pl.multiple_of(lax.rem(a + ka + 1, A) * w_o, w_o), w_o)
+                self.copies.append(start(self.got_x.at[B - 1, :, cols], self.got_z.at[ka], slots(), device("a", ka + 1)))
+
+        def finish(self):
+            cols = pl.ds(pl.multiple_of(a * w_o, w_o), w_o)
+            total = self.got_x[B - 1, :, cols].astype(F32)
+            for ka in range(A - 1):
+                self.copies[ka].wait()
+                total = total + self.got_z[ka].astype(F32)
+            self.share[...] = total.astype(BF)
+            self.gather.begin()
+
+    square_o = Square(go_ref, o_c, o_y, o_x, o_z, o_s, gather_o)
+    square_q = Square(gq_ref, q_c, q_y, q_x, q_z, q_s, gather_q)
+
+    square_o.over_c()
 
     scale = 1.0 / math.sqrt(HS)
     factor = math.log2(math.e) * scale
@@ -422,15 +651,13 @@
             d_scores = (probs * (d_probs - delta[h : h + 1, :])).astype(BF)
             d_values = d_values + nn(probs.astype(BF), d)
             d_keys = d_keys + nn(d_scores, q)
-            acc[h] = acc[h] + nn(keys_t, d_scores)
+            acc[head_block(h, tok)] += nn(keys_t, d_scores)
         for i in range(2):
             part = slice(i * tok, (i + 1) * tok)
             dkv[j, i, :, :HS] = (d_keys[part] * scale).astype(BF)
             dkv[j, i, :, HS:] = d_values[part].astype(BF)
 
     chunks = s // 2 + 1
-    per = -(-(window // CHUNK) // max(1, A - 1))
-
     def attention_chunk(j, carry):
         plain = jnp.logical_and(jnp.logical_and(j > 0, j < chunks - 1), s < 2 * A * B - 1)
 
@@ -444,20 +671,27 @@
 
         return carry
 
-    def feed_forward_step(i, carry):
-        lax.fori_loop(i * per, jnp.minimum((i + 1) * per, chunks), attention_chunk, 0)
-        for copy in down_copies(i) + up_copies(i):
-            copy.wait()
-        total_d, total_u = own_sums(i)
-        to = lax.rem(a + 1 + i, A)
-        to = ((to * B + b) * 2 + c, f)
-        zs_d[i] = total_d.astype(BF)
-        remote(zs_d.at[i], zr_d.at[i], z_d + i, to).start()
-        zs_u[i] = total_u.astype(BF)
-        remote(zs_u.at[i], zr_u.at[i], z_u + i, to).start()
+    first = 0 if head is None else min(2, A - 1)
+    steps = [functools.partial(down_step, i) for i in range(first, A - 1)]
+    steps += [functools.partial(up_step, i) for i in range(A - 2)] + [down_share]
+    if A == 4:
+        times = (1, 3, 5, 4) if head is not None else (0, 1, 2, 3, 4, 5)
+        at_chunk = dict(zip(times, steps))
+        at_chunk[2] = square_o.over_f
+        at_chunk[6 if head is not None else 7] = square_o.over_b
+    else:
+        at_chunk = {0: square_o.over_f, 1: lambda: [step() for step in steps], 2: square_o.over_b}
+
+    def chunk_and_step(j, carry):
+        @pl.when(j < chunks)
+        def _():
+            attention_chunk(j, 0)
+
+        for time, act in at_chunk.items():
+            pl.when(j == time)(lambda act=act: act() and None)
         return carry
 
-    lax.fori_loop(0, A - 1, feed_forward_step, 0)
+    lax.fori_loop(0, window // CHUNK, chunk_and_step, 0)
 
     def clear(j, carry):
         dkv[j] = jnp.zeros(dkv.shape[1:], BF)
@@ -465,154 +699,13 @@
 
     lax.fori_loop(chunks, window // CHUNK, clear, 0)
 
-    class Gather:
-        def __init__(self, share, view, planes=True):
-            self.share, self.view, self.planes = share, view, planes
-            n = B if planes else 1
-            self.z = slots(A - 1)
-            self.x = slots((n - 1) * A)
-            self.s = slots(n * A)
-            self.local = pltpu.make_async_copy(share, view(c, b, a), copy_sem.at[len(gathers)])
-            gathers.append(self)
-
-        def begin(self):
-            self.local.start()
-            mine = self.view(c, b, a)
-            self.zs = [start(self.share, mine, self.z + k, device("a", k + 1)) for k in range(A - 1)]
-            self.xs, self.cs = {}, {}
-            self.pass_on(self.share, mine, 0)
-
-        def pass_on(self, src, dst, j):
-            for kb in range(B - 1 if self.planes else 0):
-                self.xs[kb, j] = start(src, dst, self.x + kb * A + j, device("b", kb + 1))
-            self.cs[0, j] = start(src, dst, self.s + j, device("c", 1))
-
-        def from_a(self):
-            for k in range(A - 1):
-                self.zs[k].wait_recv()
-                here = self.view(c, b, lower("a", k + 1))
-                self.pass_on(here, here, k + 1)
-
-        def from_b(self):
-            for kb in range(B - 1 if self.planes else 0):
-                for j in range(A):
-                    self.xs[kb, j].wait_recv()
-                    here = self.view(c, lower("b", kb + 1), lower("a", j) if j else a)
-                    self.cs[kb + 1, j] = start(here, here, self.s + (kb + 1) * A + j, device("c", 1))
-
-        def end(self):
-            self.local.wait()
-            for copy in self.zs + list(self.xs.values()):
-                copy.wait_send()
-            for copy in self.cs.values():
-                copy.wait()
-
-    gathers = []
-
-    def view_down(c_, b_, a_):
-        return out_down.at[pl.ds(pl.multiple_of(((c_ * B + b_) * A + a_) * r_d, r_d), r_d), :]
-
-    def view_up(c_, b_, a_):
-        rows = pl.ds(pl.multiple_of(b_ * r_u, r_u), r_u)
-        return out_up.at[:, rows, pl.ds(pl.multiple_of(c_ * shard + a_ * w_u, w_u), w_u)]
-
-    w_o = half // A
-
-    def view_square(out):
-        def view(c_, b_, a_):
-            rows = pl.ds(pl.multiple_of(b_ * r_u, r_u), r_u)
-            return out.at[rows, pl.ds(pl.multiple_of(c_ * half + a_ * w_o, w_o), w_o)]
-
-        return view
-
-    gather_down = Gather(sh_d, view_down)
-    gather_up = Gather(sh_u, view_up)
-    gather_o = Gather(o_s, view_square(out_o))
-    gather_q = Gather(q_s, view_square(out_q))
-    gather_kv = Gather(kv_s, lambda c_, b_, a_: out_kv.at[c_, a_], planes=False)
-
     dkv_c_copy = start(dkv.at[:, 1 - c], dkv_c, slots(), device("c", 1))
 
-    for copy in down_copies(A - 1) + up_copies(A - 1):
-        copy.wait()
-    total_d, total_u = own_sums(A - 1)
-
-    def z_wait(i, carry):
-        to = lax.rem(a + 1 + i, A)
-        to = ((to * B + b) * 2 + c, f)
-        remote(zs_d.at[i], zr_d.at[i], z_d + i, to).wait()
-        remote(zs_u.at[i], zr_u.at[i], z_u + i, to).wait()
-        return carry
-
-    lax.fori_loop(0, A - 1, z_wait, 0)
-    for i in range(A - 1):
-        total_d = total_d + zr_d[i].astype(F32)
-        total_u = total_u + zr_u[i].astype(F32)
-    sh_d[...] = total_d.astype(BF)
-    gather_down.begin()
-    yr_u[...] = total_u.astype(BF)
-    up_y = []
-    for kf in range(F - 1):
-        up_y.append(start(yr_u.at[lax.rem(f + kf + 1, F)], sh_u.at[f], slots(), device("f", kf + 1)))
-    sh_u[f] = yr_u[f]
-
-    class Square:
-        def __init__(self, grad, got_c, got_y, got_x, got_z, share, gather):
-            self.grad, self.got_c, self.got_y, self.got_x, self.got_z = grad, got_c, got_y, got_x, got_z
-            self.share, self.gather = share, gather
-
-        def over_c(self):
-            self.copy_c = reduce_c(self.grad, self.got_c, half)
-
-        def over_f(self):
-            self.copy_c.wait()
-            reduce_y(self.grad, self.got_c, self.got_c, half)
-            self.copies = [
-                start(self.got_c.at[lax.rem(f + kf + 1, F)], self.got_y.at[kf], slots(), device("f", kf + 1)) for kf in range(F - 1)
-            ]
-
-        def over_b(self):
-            total = self.got_c[f].astype(F32)
-            for kf in range(F - 1):
-                self.copies[kf].wait()
-                total = total + self.got_y[kf].astype(F32)
-            self.got_y[F - 1] = total.astype(BF)
-            self.copies = []
-            for kb in range(B - 1):
-                rows = pl.ds(pl.multiple_of(lax.rem(b + kb + 1, B) * r_u, r_u), r_u)
-                self.copies.append(start(self.got_y.at[F - 1, rows, :], self.got_x.at[kb], slots(), device("b", kb + 1)))
-
-        def over_a(self):
-            rows = pl.ds(pl.multiple_of(b * r_u, r_u), r_u)
-            total = self.got_y[F - 1, rows, :].astype(F32)
-            for kb in range(B - 1):
-                self.copies[kb].wait()
-                total = total + self.got_x[kb].astype(F32)
-            self.got_x[B - 1] = total.astype(BF)
-            self.copies = []
-            for ka in range(A - 1):
-                cols = pl.ds(pl.multiple_of(lax.rem(a + ka + 1, A) * w_o, w_o), w_o)
-                self.copies.append(start(self.got_x.at[B - 1, :, cols], self.got_z.at[ka], slots(), device("a", ka + 1)))
-
-        def finish(self):
-            cols = pl.ds(pl.multiple_of(a * w_o, w_o), w_o)
-            total = self.got_x[B - 1, :, cols].astype(F32)
-            for ka in range(A - 1):
-                self.copies[ka].wait()
-                total = total + self.got_z[ka].astype(F32)
-            self.share[...] = total.astype(BF)
-            self.gather.begin()
-
-    square_o = Square(go_ref, o_c, o_y, o_x, o_z, o_s, gather_o)
-    square_o.copy_c = o_c_copy
-    square_q = Square(gq_ref, q_c, q_y, q_x, q_z, q_s, gather_q)
-
-    square_o.over_f()
 
     if head is not None:
         finish_output()
     for h in range(H):
-        dq[:, h * HS : (h + 1) * HS] = (acc[h] * scale).T.astype(BF)
+        dq[:, h * HS : (h + 1) * HS] = (acc[head_block(h, tok)] * scale).T.astype(BF)
     n_rows = 128
 
     def query_grad(i, carry):
@@ -638,11 +731,9 @@
         for j in range(A):
             x_kv.append(start(dkv_c.at[j * B + other], dkv_x.at[kb, j], slots(), device("b", kb + 1)))
 
-    square_o.over_b()
-    for copy in up_y:
-        copy.wait()
-    gather_up.begin()
+    up_step(A - 2)
     gather_down.from_a()
+    up_share()
     square_q.over_f()
 
     for copy in x_kv:
@@ -664,9 +755,9 @@
             to = (((a - k) * B + b) * 2 + c, f)
             remote(dkv_x.at[0, jnp.maximum(a - k, 0)], dkv_z.at[k - 1], z_kv + k - 1, to).start()
 
+    up_gather()
     square_o.over_a()
     square_q.over_b()
-    gather_up.from_a()
 
     total = dkv_x[0, a].astype(F32)
     d_kv[...] = total
@@ -711,7 +802,7 @@
                 gkv_ref[ci, fi, i, r_kv:, :] = block.astype(BF)
     kv_c_copy = start(gkv_ref.at[1 - c], kv_c, slots(), device("c", 1))
 
-    square_o.finish()
+    gather_up.from_a()
     for i in range(D // n_cols):
         cols = slice(i * n_cols, (i + 1) * n_cols)
         grad_tokens[:, cols] = dres_ref[:, cols] + inv_ref[...] * (
@@ -721,14 +812,14 @@
     kv_c_copy.wait()
     kv_c[...] = (kv_c[...].astype(F32) + gkv_ref[c].astype(F32)).astype(BF)
     kv_f = [start(kv_c.at[lax.rem(f + kf + 1, F)], kv_y.at[kf], slots(), device("f", kf + 1)) for kf in range(F - 1)]
-    gather_down.from_b()
-    gather_o.from_a()
+    square_o.finish()
     total = kv_c[f].astype(F32)
     for kf in range(F - 1):
         kv_f[kf].wait()
         total = total + kv_y[kf].astype(F32)
     kv_y[F - 1] = total.astype(BF)
     kv_b = [start(kv_y.at[F - 1], kv_x.at[kb], slots(), device("b", kb + 1)) for kb in range(B - 1)]
+    gather_o.from_a()
     square_q.finish()
     total = kv_y[F - 1].astype(F32)
     for kb in range(B - 1):
@@ -736,7 +827,7 @@
         total = total + kv_x[kb].astype(F32)
     kv_x[B - 1] = total.astype(BF)
     kv_a = [start(kv_x.at[B - 1, lax.rem(a + ka + 1, A)], kv_z.at[ka], slots(), device("a", ka + 1)) for ka in range(A - 1)]
-    gather_up.from_b()
+    gather_down.from_b()
     total = kv_x[B - 1, a].astype(F32)
     for ka in range(A - 1):
         kv_a[ka].wait()
@@ -744,8 +835,9 @@
     kv_s[...] = total.astype(BF)
     gather_kv.begin()
     gather_q.from_a()
+    gather_up.from_b()
+    gather_kv.from_a()
     gather_o.from_b()
-    gather_kv.from_a()
     gather_q.from_b()
     for gather in gathers:
         gather.end()
@@ -763,8 +855,8 @@
         return pltpu.VMEM(shape, BF)
 
     square = [low(F, own_rows, half), low(F, own_rows, half), low(B, r_u, half), low(A - 1, r_u, w_o), low(r_u, w_o)]
-    n_sems = extra + 2 * (A * (B - 1) + A - 1) + 4 * (A - 1 + (B - 1) * A + B * A) + (A - 1 + A)
-    n_sems += 2 * (F + B + A) + F + (B - 1) * A + A + F + B + A + 8
+    n_sems = extra + 2 * (A * (B - 1) + A - 1) + 4 * (A + (B - 1) * A + B * A) + 2 * A
+    n_sems += 2 * (F + B + A) + 2 * F + (B - 1) * A + A + F + B + A + 8
     outs = (
         jax.ShapeDtypeStruct((2 * shard, D), BF),
         jax.ShapeDtypeStruct((F, own_rows, 2 * shard), BF),
@@ -774,7 +866,7 @@
         jax.ShapeDtypeStruct((tok, D), F32),
     )
     scratch = [
-        pltpu.VMEM((H, HS, tok), F32),
+        pltpu.VMEM((2 * HS, H // 2 * tok), F32),
         pltpu.VMEM((H, tok), F32),
         low(tok, D),
         low(A * B, 2, tok, 2 * HS),
@@ -828,7 +920,8 @@
 
 
 HEAD_IN = (
-    "ends",
+    "lengths",
+    "groups",
     "tokens",
     "gains_in",
     "wk_in",
@@ -873,9 +966,8 @@
     "out_c",
     "out_y",
     "out_r",
-    "top",
-    "total",
     "loc_sem",
+    "ends",
 )
 
 
@@ -913,9 +1005,18 @@
     wk_f = to_f(lambda kf: r.wk_in.at[mine_half, :], lambda kf: r.wkv_ref.at[full_half, :HS])
     wv_f = to_f(lambda kf: r.wv_in.at[mine_half, :], lambda kf: r.wkv_ref.at[full_half, HS:])
     wq_f = to_f(lambda kf: r.wq_in.at[mine_half, :], lambda kf: r.wq_ref.at[full_half, :])
-    wo_f = to_f(lambda kf: r.wo_in.at[mine_half, :], lambda kf: r.wo_ref.at[full_half, :])
+    part, up_part = half // B, own_rows // B
+
+    def wo_rows(f_, c_, b_):
+        return span(((f_ * 2 + c_) * B + b_) * part, part)
+
+    def up_rows(f_, b_):
+        return span((f_ * B + b_) * up_part, up_part)
+
+    wo_f = to_f(lambda kf: r.wo_in.at[span((c * B + b) * part, part), :], lambda kf: r.wo_ref.at[wo_rows(f, c, b), :])
     up_f = to_f(
-        lambda kf: r.up_in.at[:, span((lax.rem(f + kf, F) * 2 + c) * shard, shard)], lambda kf: r.up_ref.at[mine, :]
+        lambda kf: r.up_in.at[span(b * up_part, up_part), span((lax.rem(f + kf, F) * 2 + c) * shard, shard)],
+        lambda kf: r.up_ref.at[up_rows(f, b), :],
     )
     cot_f = to_f(lambda kf: r.cot_in, lambda kf: r.cot_all.at[kf, :tok])
     cot_c = [start(r.cot_in, r.cot_all.at[0, tok:], sibling)]
@@ -943,6 +1044,19 @@
             passed.append(start(ref.at[rows, cols], ref.at[rows, cols], sibling))
         return passed
 
+    def along_b(copies, ref, rows):
+        passed = []
+        for kf in range(1, F):
+            copies[kf - 1].wait_recv()
+            here = ref.at[rows(lower("f", kf)), :]
+            passed += [start(here, here, device("b", kb)) for kb in range(1, B)]
+        return passed
+
+    group = r.groups[f]
+    end = jnp.int32(0)
+    for i in range(r.ends.shape[0]):
+        end = end + r.lengths[group, i]
+        r.ends[i] = end
     n_rows = 64
 
     def unit_rows(i, carry):
@@ -1033,34 +1147,38 @@
             pass_on(k)
 
         guarded(k, a - k >= 0, arrived)
+    wo_b = along_b(wo_f, r.wo_ref, lambda f_: wo_rows(f_, c, b))
 
     factor = math.log2(math.e) / math.sqrt(HS)
-    r.top[...] = jnp.full(r.top.shape, -3e38, F32)
-    r.total[...] = jnp.zeros(r.total.shape, F32)
-    r.acc[...] = jnp.zeros(r.acc.shape, F32)
-    pos = s * tok + lax.broadcasted_iota(jnp.int32, (1, tok), 1)
-    begin = jnp.zeros((1, tok), jnp.int32)
+    top, mixed, total = r.dres_ref, r.res_ref, r.acc
+    top[...] = jnp.full(top.shape, -3e38, F32)
+    mixed[...] = jnp.zeros(mixed.shape, F32)
+    total[...] = jnp.zeros(total.shape, F32)
+    pos = s * tok + lax.broadcasted_iota(jnp.int32, (tok, 1), 0)
+    begin = jnp.zeros((tok, 1), jnp.int32)
     for i in range(r.ends.shape[0]):
         begin = jnp.maximum(begin, jnp.where(r.ends[i] <= pos, r.ends[i], 0))
 
     def step(j, masked):
         rows = span(j * CHUNK, CHUNK)
         keys = kv[rows, :HS]
-        values_t = kv[rows, HS:].T
+        values = jnp.concatenate([kv[rows, HS:], jnp.ones((CHUNK, HS), BF)], axis=1)
         if masked:
-            at = j * CHUNK + lax.broadcasted_iota(jnp.int32, (CHUNK, tok), 0)
+            at = j * CHUNK + lax.broadcasted_iota(jnp.int32, (tok, CHUNK), 1)
             mask = jnp.logical_and(at >= begin, at <= pos)
         for h in range(H):
-            scores = nt(keys, r.q_ref[:, h * HS : (h + 1) * HS])
+            cols = slice(h * HS, (h + 1) * HS)
+            scores = nt(r.q_ref[:, cols], keys)
             if masked:
                 scores = jnp.where(mask, scores, NEG)
-            old = r.top[h : h + 1, :]
-            new = jnp.maximum(old, jnp.max(scores, axis=0, keepdims=True) * factor)
+            old = top[:, cols]
+            new = jnp.maximum(old, jnp.max(scores, axis=1, keepdims=True) * factor)
             shrink = jnp.exp2(old - new)
-            probs = jnp.exp2(scores * factor - new)
-            r.total[h : h + 1, :] = r.total[h : h + 1, :] * shrink + jnp.sum(probs, axis=0, keepdims=True)
-            r.acc[h] = r.acc[h] * shrink + nn(values_t, probs.astype(BF))
-            r.top[h : h + 1, :] = new
+            probs = jnp.exp2(scores * factor - jnp.concatenate([new] * (CHUNK // HS), axis=1))
+            both = nn(probs.astype(BF), values)
+            mixed[:, cols] = mixed[:, cols] * shrink + both[:, :HS]
+            total[:, cols] = total[:, cols] * shrink + both[:, HS:]
+            top[:, cols] = new
 
     last = s // 2
     c_copy(0, 0).wait_recv()
@@ -1078,6 +1196,8 @@
             if kb or k:
                 guarded(k, a - k >= 0, c_copy(kb, k).wait_recv)
 
+    up_b = along_b(up_f, r.up_ref, lambda f_: up_rows(f_, b))
+
     def attention_chunk(j, carry):
         plain = jnp.logical_and(j > 0, s < 2 * A * B - 1)
 
@@ -1093,12 +1213,17 @@
 
     lax.fori_loop(0, last, attention_chunk, 0)
     for h in range(H):
-        mixed = r.acc[h] * (1.0 / r.total[h : h + 1, :])
-        r.att_ref[:, h * HS : (h + 1) * HS] = mixed.T.astype(BF)
-    r.lse_ref[...] = r.top[...] + jnp.log2(r.total[...])
+        cols = slice(h * HS, (h + 1) * HS)
+        r.att_ref[:, cols] = (mixed[:, cols] * (1.0 / total[:, cols])).astype(BF)
+        r.lse_ref[h : h + 1, :] = (top[:, cols] + jnp.log2(total[:, cols])).T[0:1, :]
 
     local[1].wait()
-    wo_c = weight_halves(wo_f, r.wo_ref, slice(0, D))
+    wo_c = []
+    for copy in wo_b:
+        copy.wait_recv()
+    for kf in range(1, F):
+        here = r.wo_ref.at[span((lower("f", kf) * 2 + c) * half, half), :]
+        wo_c.append(start(here, here, sibling))
     for copy in wo_c:
         copy.wait_recv()
     squares = jnp.zeros((tok, 1), F32)
@@ -1121,7 +1246,7 @@
     local[2].wait()
     local[3].wait()
     local[4].wait()
-    for copy in up_f:
+    for copy in up_b:
         copy.wait_recv()
     for kf in range(1, F):
         cot_f[kf - 1].wait_recv()
@@ -1158,10 +1283,35 @@
 
         lax.fori_loop(0, tok // n_rows, rows_sum, 0)
 
+    n_out = 128
+
+    def down_grad(kf):
+        def rows_of(i, carry):
+            cols = span(i * n_out, n_out)
+            grad = tn(r.hid_all[kf, :, cols], r.cot_all[kf])
+            r.gd_ref[cols, :] = (grad + r.gd_ref[cols, :].astype(F32) if kf else grad).astype(BF)
+            return carry
+
+        lax.fori_loop(0, shard // n_out, rows_of, 0)
+
+    def up_grad(kf):
+        def rows_of(i, carry):
+            cols = span(i * n_out, n_out)
+            rows = span(lax.rem(i, own_rows // n_out) * n_out, n_out)
+            at = i // (own_rows // n_out)
+            grad = tn(r.n2_all[kf, :, cols], r.dp_all[kf])
+            r.gu_ref[at, rows, :] = (grad + r.gu_ref[at, rows, :].astype(F32) if kf else grad).astype(BF)
+            return carry
+
+        lax.fori_loop(0, D // n_out, rows_of, 0)
+
     back_copies, out_copies, back_back, out_back = [None] * F, [None] * F, [], []
     n2_c[0].wait_recv()
     cot_c[0].wait_recv()
     back_copies[0] = feed_forward(0)
+    down_grad(0)
+    up_grad(0)
+    out_copies[0] = out_part(0)
     for kf in range(1, F):
         n2_f[kf - 1].wait_recv()
         n2_c.append(start(r.n2_all.at[kf, :tok], r.n2_all.at[kf, tok:], sibling))
@@ -1169,38 +1319,22 @@
         n2_c[kf].wait_recv()
         cot_c[kf].wait_recv()
         back_copies[kf] = feed_forward(kf)
-        out_copies[kf] = out_part(kf)
+        if kf == F - 1:
+            down_grad(kf)
+            x.send_down(0, A)
         back_copies[kf].wait_recv()
         chip_sum(kf, r.back_s, r.back_c, r.back_y)
         back_back.append(start(r.back_y.at[kf - 1], r.back_r.at[kf - 1], device("f", F - kf)))
-
-    n_out = 128
-
-    def down_grad(i, carry):
-        cols = span(i * n_out, n_out)
-        r.gd_ref[cols, :] = sum(tn(r.hid_all[kf, :, cols], r.cot_all[kf]) for kf in range(F)).astype(BF)
-        return carry
-
-    lax.fori_loop(0, shard // n_out, down_grad, 0)
-    x.send_down(0, 1)
-
-    def up_grad(i, carry):
-        cols = span(i * n_out, n_out)
-        rows = span(lax.rem(i, own_rows // n_out) * n_out, n_out)
-        grad = sum(tn(r.n2_all[kf, :, cols], r.dp_all[kf]) for kf in range(F))
-        r.gu_ref[i // (own_rows // n_out), rows, :] = grad.astype(BF)
-        return carry
-
-    lax.fori_loop(0, D // n_out, up_grad, 0)
-    x.send_up(0, 1)
-    for i in range(1, A):
-        x.send_down(i, i + 1)
-        x.send_up(i, i + 1)
+        if kf < F - 1:
+            down_grad(kf)
+        up_grad(kf)
+        out_copies[kf] = out_part(kf)
+    x.send_up(0, A)
     for kf in range(1, F):
         out_copies[kf].wait_recv()
         chip_sum(kf, r.out_s, r.out_c, r.out_y)
         out_back.append(start(r.out_y.at[kf - 1], r.out_r.at[kf - 1], device("f", F - kf)))
-    out_copies[0] = out_part(0)
+    x.down_step(0)
 
     back_copies[0].wait_recv()
     for copy in back_back:
@@ -1237,6 +1371,8 @@
         return carry
 
     lax.fori_loop(0, D // n_out, out_grad, 0)
+    if A > 2:
+        x.down_step(1)
 
     def finish_output():
         out_copies[0].wait_recv()
@@ -1288,7 +1424,7 @@
 }
 
 
-def layer_shapes(dims, tok, D, shard, window):
+def layer_shapes(dims, tok, D, shard, window, sequences):
     A, B, F = dims
     own_rows = D // F
     outs, scratch = tail_shapes(dims, tok, D, shard, window, 16 * F + A - 1 + (B - 1) * A + B * A)
@@ -1328,12 +1464,11 @@
         low(tok, D),
         *pair,
         *pair,
-        wide(H, tok),
-        wide(H, tok),
         pltpu.SemaphoreType.DMA((7,)),
+        pltpu.SMEM((sequences,), jnp.int32),
     ]
     sizes = dict(zip(HEAD_SCRATCH + TAIL_SCRATCH, first + scratch))
-    fits = all(sizes[k].shape == sizes[AGAIN[k]].shape for k in ("gq_ref", "dn1", "dq")) and own_rows == 2 * tok
+    fits = all(sizes[k].shape == sizes[AGAIN[k]].shape for k in ("gq_ref", "dn1", "dq")) and tok == 2 * HS and own_rows == 2 * tok
     scratch = [ref for name, ref in zip(TAIL_SCRATCH, scratch) if name not in AGAIN]
     fits = fits and vmem_bytes(first + scratch) + 4 * 2**20 < LIMIT
     return outs + (jax.ShapeDtypeStruct((tok, D), BF),), first + scratch, fits
@@ -1350,20 +1485,20 @@
     return total
 
 
-def layer(dims, ends, tokens, gains, w_key, w_value, cotangent, w_query, w_out, w_up, w_down, outs, scratch):
+def layer(dims, lengths, groups, tokens, gains, w_key, w_value, cotangent, w_query, w_out, w_up, w_down, outs, scratch):
     tok, D = tokens.shape
     hbm = pl.BlockSpec(memory_space=pltpu.HBM)
     names = HEAD_IN + TAIL_OUT[:5] + ("grad_hbm", "out_hbm") + HEAD_SCRATCH + tuple(n for n in TAIL_SCRATCH if n not in AGAIN)
     return pl.pallas_call(
         functools.partial(tail_kernel, dims, head, names),
         out_shape=outs,
-        in_specs=[SMEM] + [VMEM] * 4 + [hbm] * 5,
+        in_specs=[SMEM] * 2 + [VMEM] * 4 + [hbm] * 5,
         out_specs=(hbm,) * 7,
         scratch_shapes=scratch,
         compiler_params=pltpu.CompilerParams(vmem_limit_bytes=LIMIT, collective_id=2, has_side_effects=True),
         cost_estimate=pl.CostEstimate(flops=2**35, bytes_accessed=2**25, transcendentals=2**24),
         name="layer",
-    )(ends, tokens, gains, w_key, w_value, cotangent, w_query, w_out, w_up, w_down)
+    )(lengths, groups, tokens, gains, w_key, w_value, cotangent, w_query, w_out, w_up, w_down)
 
 
 def after(value, *others):
@@ -1461,6 +1596,28 @@
     seq_parts = A * B * C
     shard = FF // (2 * F)
 
+    outs, scratch, fits = layer_shapes((A, B, F), tok, D, shard, seq_parts * tok, seq_lengths.shape[1])
+    if fits:
+        row = lax.broadcasted_iota(jnp.int32, (16, own_rows), 0)
+        gains = jnp.where(row == 0, gain_attn[None], gain_ffn[None])
+        *grads, grad_tokens, output = layer(
+            (A, B, F),
+            seq_lengths,
+            group_of_shard,
+            tokens[0],
+            gains,
+            w_key,
+            w_value,
+            cotangent[0],
+            w_query,
+            w_out,
+            w_up,
+            w_down,
+            outs,
+            scratch,
+        )
+        return results(output, grad_tokens, *grads)
+
     group = lax.dynamic_index_in_dim(group_of_shard, g.f, 0, keepdims=False)
     lengths = lax.dynamic_index_in_dim(seq_lengths, group, 0, keepdims=False)
     running, ends = jnp.int32(0), []
@@ -1468,14 +1625,6 @@
         running = running + lengths[i]
         ends.append(running)
     scal = jnp.stack([g.s.astype(jnp.int32), *ends])
-
-    outs, scratch, fits = layer_shapes((A, B, F), tok, D, shard, seq_parts * tok)
-    if fits:
-        gains = jnp.pad(jnp.stack([gain_attn, gain_ffn]), ((0, 14), (0, 0)))
-        *grads, grad_tokens, output = layer(
-            (A, B, F), scal[1:], tokens[0], gains, w_key, w_value, cotangent[0], w_query, w_out, w_up, w_down, outs, scratch
-        )
-        return results(output, grad_tokens, *grads)
 
     gains = jnp.stack([gain_attn, gain_ffn])
     full_gains = g.gather(gains, "f").transpose(1, 0, 2).reshape(2, D).astype(F32)
@@ -1598,24 +1747,74 @@
     return results(output, grad_tokens, down_all, up_all, out_all, query_all, kv_all)
 
 
+def widen_kernel(
+    low_ref, grad_ref, down_ref, up_ref, o_ref, q_ref, kv_ref, output, grad_tokens, grad_down, grad_up, grad_o, grad_q, grad_k, grad_v, gains
+):
+    output[0] = low_ref[...]
+    grad_tokens[0] = grad_ref[...]
+    grad_down[...] = down_ref[...].astype(F32)
+    width = up_ref.shape[2]
+    for i in range(up_ref.shape[0]):
+        grad_up[:, i * width : (i + 1) * width] = up_ref[i].astype(F32)
+    grad_o[...] = o_ref[...].astype(F32)
+    grad_q[...] = q_ref[...].astype(F32)
+
+    @pl.when(pl.program_id(0) == 0)
+    def _():
+        rows = kv_ref.shape[2] - 16
+        for i in range(kv_ref.shape[1]):
+            grad_k[i * rows : (i + 1) * rows, :] = kv_ref[0, i, :rows, :].astype(F32)
+            grad_v[i * rows : (i + 1) * rows, :] = kv_ref[1, i, :rows, :].astype(F32)
+        for i in range(2):
+            gains[i] = kv_ref[i, 0, rows:, :].astype(F32)
+
+
 def results(output, grad_tokens, down_all, up_all, out_all, query_all, kv_all):
-    F, own_rows = up_all.shape[:2]
-    grad_w_up = jnp.concatenate([up_all[i].astype(F32) for i in range(F)], axis=1)
-    r_kv = own_rows // kv_all.shape[1]
-    grad_kv = kv_all[:, :, :r_kv].astype(F32).reshape(2, own_rows, HS)
-    gain_grads = kv_all[:, 0, r_kv : r_kv + own_rows // 128].astype(F32).reshape(2, own_rows)
-    return (
-        output[None],
-        grad_tokens[None],
-        gain_grads[0],
-        query_all.astype(F32),
-        grad_kv[0],
-        grad_kv[1],
-        out_all.astype(F32),
-        gain_grads[1],
-        grad_w_up,
-        down_all.astype(F32),
-    )
+    tok, D = output.shape
+    F, own_rows, width = up_all.shape
+    steps = max(1, own_rows // 256)
+
+    def rows(n, cols):
+        return pl.BlockSpec((n // steps, cols), lambda i: (i, 0))
+
+    def whole(*shape):
+        return pl.BlockSpec(shape, lambda i: (0,) * len(shape))
+
+    def first(n, cols):
+        return pl.BlockSpec((1, n // steps, cols), lambda i: (0, i, 0))
+
+    down_rows = down_all.shape[0]
+    shapes = [(down_rows, D), (own_rows, F * width), (own_rows, D), (own_rows, D), (own_rows, HS), (own_rows, HS), (2, 16, HS)]
+    out, grad_tokens, down, up, o, q, k, v, gains = pl.pallas_call(
+        widen_kernel,
+        grid=(steps,),
+        out_shape=[jax.ShapeDtypeStruct((1, tok, D), BF), jax.ShapeDtypeStruct((1, tok, D), F32)]
+        + [jax.ShapeDtypeStruct(shape, F32) for shape in shapes],
+        in_specs=[
+            rows(tok, D),
+            rows(tok, D),
+            rows(down_rows, D),
+            pl.BlockSpec((F, own_rows // steps, width), lambda i: (0, i, 0)),
+            rows(own_rows, D),
+            rows(own_rows, D),
+            whole(*kv_all.shape),
+        ],
+        out_specs=[
+            first(tok, D),
+            first(tok, D),
+            rows(down_rows, D),
+            rows(own_rows, F * width),
+            rows(own_rows, D),
+            rows(own_rows, D),
+            whole(own_rows, HS),
+            whole(own_rows, HS),
+            whole(2, 16, HS),
+        ],
+        compiler_params=pltpu.CompilerParams(vmem_limit_bytes=LIMIT),
+        name="widen",
+    )(output, grad_tokens, down_all, up_all, out_all, query_all, kv_all)
+    gains = gains[:, : own_rows // HS].reshape(2, own_rows)
+    return out, grad_tokens, gains[0], q, k, v, o, gains[1], up, down
 
 
 def solution(mesh):

time: 293 us -> 236 us (0.81)
  Pallas kernels: 265 us -> 232 us
  other arithmetic: 14 us -> 1.38 us
  local copies, waits for them, and re-layouts: 9.21 us -> 1.27 us
  between operations: 4.6 us -> 0.66 us
    pallas_call x1, Pallas kernels: 265 us -> 221 us  [layer(): pl.pallas_call(functools.partial(tail_kernel, dims, head, names), out_sha...]
    pallas_call x0 -> x1, Pallas kernels: none -> 11.3 us  [results(): pl.pallas_call(widen_kernel, grid=(steps,), out_shape=[jax.ShapeDtypeStru...]
    convert_element_type x5 -> x0, other arithmetic: 7.64 us -> none  [the longest x1 4.47 us: results(): down_all.astype(F32)]
    concatenate x1 -> x0, other arithmetic: 4.48 us -> none  [results(): jnp.concatenate([up_all[i].astype(F32) for i in range(F)], axis=1)]
where the time goes in v1:
time: 236 us; the launch traced here: 235 us
  Pallas kernels  232 us (98%)
    pallas_call x1, Pallas kernels, layer(): pl.pallas_call(functools.partial(tail_kernel, dims, head, names), out_sha...  221 us
    pallas_call x1, Pallas kernels, results(): pl.pallas_call(widen_kernel, grid=(steps,), out_shape=[jax.ShapeDtypeStru...  11.3 us

profile of v1, /device:TPU:0, one launch (start us, length us, event | category | flops | bytes accessed | tf_op | source)
XLA Modules:
  0.0 235.3 jit_solution(12986405889298568314)
XLA Ops:
  0.7 1.4 broadcast_select_fusion.refs_3_
  2.0 220.7 %layer.1 = (bf16[2048,1024]{1,0:T(8,128)(2,1)}, bf16[2,512,2048]{2,1,0:T(8,128)(2,1)}, bf16[512,1024]{1,0:T(8,128)(2,1)}, bf16[512,1024]{1,0:T(8,128)(2,1)}, bf1...) custom-call(s32[2,3]{1,0:T(2,128)} %refs_0_.1, s32[2]{0:T(128)} %refs_1_.1, ...), custom_call_target="tpu_custom_call" | custom-call | flops 34359738368 | bytes 33554432 | tf_op jit(solution)/shard_map/layer/pallas_call | solution.py:1492
  222.7 11.3 %widen.1 = (bf16[1,256,1024]{2,1,0:T(8,128)(2,1)}, f32[1,256,1024]{2,1,0:T(8,128)}, f32[2048,1024]{1,0:T(8,128)}, f32[512,4096]{1,0:T(8,128)}, f32[512,1024]{1,0...) custom-call(bf16[256,1024]{1,0:T(8,128)(2,1)} %get-tuple-element.26.low_ref, ...), custom_call_target="tpu_custom_call" | custom-call | tf_op jit(solution)/shard_map/widen/pallas_call | solution.py:1788
  234.0 1.3 slice_bitcast_fusion
  (1 shorter events, 0.0 us)

commit v2 on v1

--- a/solution.py
+++ b/solution.py
@@ -542,7 +542,7 @@
     else:
         own = types.SimpleNamespace(
             A=A, B=B, F=F, a=a, b=b, c=c, f=f, s=s, slots=slots, remote=remote, device=device, lower=lower,
-            send_down=send_down, send_up=send_up, down_step=down_step,
+            send_down=send_down, send_up=send_up, down_step=down_step, offset=offset, order=order,
         )
         finish_output, finish_head = head(r, own)
 
@@ -671,16 +671,15 @@
 
         return carry
 
-    first = 0 if head is None else min(2, A - 1)
+    first = 0 if head is None else min(3, A - 1)
     steps = [functools.partial(down_step, i) for i in range(first, A - 1)]
-    steps += [functools.partial(up_step, i) for i in range(A - 2)] + [down_share]
+    steps += [functools.partial(up_step, i) for i in range(A - 2)] + [down_share, square_o.over_b]
     if A == 4:
-        times = (1, 3, 5, 4) if head is not None else (0, 1, 2, 3, 4, 5)
+        times = (3, 5, 6, 7) if head is not None else (0, 1, 2, 3, 4, 5, 6)
         at_chunk = dict(zip(times, steps))
-        at_chunk[2] = square_o.over_f
-        at_chunk[6 if head is not None else 7] = square_o.over_b
+        at_chunk[2 if head is not None else 7] = square_o.over_f
     else:
-        at_chunk = {0: square_o.over_f, 1: lambda: [step() for step in steps], 2: square_o.over_b}
+        at_chunk = {0: square_o.over_f, 1: lambda: [step() for step in steps]}
 
     def chunk_and_step(j, carry):
         @pl.when(j < chunks)
@@ -732,9 +731,13 @@
             x_kv.append(start(dkv_c.at[j * B + other], dkv_x.at[kb, j], slots(), device("b", kb + 1)))
 
     up_step(A - 2)
-    gather_down.from_a()
+    square_q.over_f()
+    gather_down.from_a((0,))
     up_share()
-    square_q.over_f()
+    square_q.over_b()
+    for i in range(1, len(bits)):
+        gather_down.from_a((i,))
+    square_o.over_a()
 
     for copy in x_kv:
         copy.wait()
@@ -756,8 +759,6 @@
             remote(dkv_x.at[0, jnp.maximum(a - k, 0)], dkv_z.at[k - 1], z_kv + k - 1, to).start()
 
     up_gather()
-    square_o.over_a()
-    square_q.over_b()
 
     total = dkv_x[0, a].astype(F32)
     d_kv[...] = total
@@ -802,39 +803,43 @@
                 gkv_ref[ci, fi, i, r_kv:, :] = block.astype(BF)
     kv_c_copy = start(gkv_ref.at[1 - c], kv_c, slots(), device("c", 1))
 
-    gather_up.from_a()
+    square_q.over_a()
     for i in range(D // n_cols):
         cols = slice(i * n_cols, (i + 1) * n_cols)
         grad_tokens[:, cols] = dres_ref[:, cols] + inv_ref[...] * (
             dn1[:, cols] * gain_ref[:, cols] - tok_ref[:, cols].astype(F32) * inv_ref[...] * mean
         )
-    square_q.over_a()
     kv_c_copy.wait()
     kv_c[...] = (kv_c[...].astype(F32) + gkv_ref[c].astype(F32)).astype(BF)
     kv_f = [start(kv_c.at[lax.rem(f + kf + 1, F)], kv_y.at[kf], slots(), device("f", kf + 1)) for kf in range(F - 1)]
     square_o.finish()
+    gather_up.from_a((0,))
     total = kv_c[f].astype(F32)
     for kf in range(F - 1):
         kv_f[kf].wait()
         total = total + kv_y[kf].astype(F32)
     kv_y[F - 1] = total.astype(BF)
     kv_b = [start(kv_y.at[F - 1], kv_x.at[kb], slots(), device("b", kb + 1)) for kb in range(B - 1)]
-    gather_o.from_a()
     square_q.finish()
+    for i in range(1, len(bits)):
+        gather_up.from_a((i,))
     total = kv_y[F - 1].astype(F32)
     for kb in range(B - 1):
         kv_b[kb].wait()
         total = total + kv_x[kb].astype(F32)
     kv_x[B - 1] = total.astype(BF)
     kv_a = [start(kv_x.at[B - 1, lax.rem(a + ka + 1, A)], kv_z.at[ka], slots(), device("a", ka + 1)) for ka in range(A - 1)]
-    gather_down.from_b()
+    gather_o.from_a()
+    gather_q.from_a((0,))
     total = kv_x[B - 1, a].astype(F32)
     for ka in range(A - 1):
         kv_a[ka].wait()
         total = total + kv_z[ka].astype(F32)
     kv_s[...] = total.astype(BF)
     gather_kv.begin()
-    gather_q.from_a()
+    for i in range(1, len(bits)):
+        gather_q.from_a((i,))
+    gather_down.from_b()
     gather_up.from_b()
     gather_kv.from_a()
     gather_o.from_b()
@@ -1122,6 +1127,13 @@
 
     pass_on(0)
 
+    def from_a(k):
+        z_copies[k - 1].wait_recv()
+        pass_on(k)
+
+    if A > 2:
+        guarded(1, a >= 1, functools.partial(from_a, 1))
+
     local[0].wait()
     wq_c = weight_halves(wq_f, r.wq_ref, slice(0, D))
     for copy in wq_c:
@@ -1140,13 +1152,8 @@
 
     columns(D, query_cols)
 
-    for k in range(1, A):
-
-        def arrived(k=k):
-            z_copies[k - 1].wait_recv()
-            pass_on(k)
-
-        guarded(k, a - k >= 0, arrived)
+    for k in range(2 if A > 2 else 1, A):
+        guarded(k, a - k >= 0, functools.partial(from_a, k))
     wo_b = along_b(wo_f, r.wo_ref, lambda f_: wo_rows(f_, c, b))
 
     factor = math.log2(math.e) / math.sqrt(HS)
@@ -1183,20 +1190,45 @@
     last = s // 2
     c_copy(0, 0).wait_recv()
     step(last, True)
-    for kb in range(1, B):
-        for k in range(A):
-
-            def arrived(kb=kb, k=k):
-                x_copy(kb, k).wait_recv()
-                c_copy(kb, k).start()
-
-            guarded(k, a - k >= 0, arrived)
-    for kb in range(B):
-        for k in range(A):
+
+    def from_b(k):
+        for kb in range(1, B):
+            x_copy(kb, k).wait_recv()
+            c_copy(kb, k).start()
+
+    def from_c(k):
+        for kb in range(B):
             if kb or k:
-                guarded(k, a - k >= 0, c_copy(kb, k).wait_recv)
-
-    up_b = along_b(up_f, r.up_ref, lambda f_: up_rows(f_, b))
+                c_copy(kb, k).wait_recv()
+
+    wo_c, up_b = [], []
+    for kf in range(1, F):
+        here = r.wo_ref.at[span((lower("f", kf) * 2 + c) * half, half), :]
+        wo_c.append(remote(here, here, slots(), sibling))
+        here = r.up_ref.at[up_rows(lower("f", kf), b), :]
+        up_b += [remote(here, here, slots(), device("b", kb)) for kb in range(1, B)]
+    sent.extend(wo_c + up_b)
+
+    def pass_weights():
+        for copy in wo_b:
+            copy.wait_recv()
+        for copy in wo_c:
+            copy.start()
+        for copy in up_f:
+            copy.wait_recv()
+        for copy in up_b:
+            copy.start()
+
+    from_b(0)
+    guarded(1, a >= 1, functools.partial(from_b, 1))
+    from_c(0)
+
+    def begin_group(k):
+        for later in range(2, A) if k == 1 else ():
+            guarded(later, a - later >= 0, functools.partial(from_b, later))
+        from_c(k)
+        if k == 2:
+            pass_weights()
 
     def attention_chunk(j, carry):
         plain = jnp.logical_and(j > 0, s < 2 * A * B - 1)
@@ -1211,19 +1243,20 @@
 
         return carry
 
-    lax.fori_loop(0, last, attention_chunk, 0)
+    def attention_part(i, carry):
+        j = last - 1 - i
+        for k in range(1, A):
+            pl.when(j == (a - k) * B + B - 1)(functools.partial(begin_group, k))
+        return attention_chunk(j, carry)
+
+    lax.fori_loop(0, last, attention_part, 0)
+    guarded(1, a < 2, pass_weights)
     for h in range(H):
         cols = slice(h * HS, (h + 1) * HS)
         r.att_ref[:, cols] = (mixed[:, cols] * (1.0 / total[:, cols])).astype(BF)
         r.lse_ref[h : h + 1, :] = (top[:, cols] + jnp.log2(total[:, cols])).T[0:1, :]
 
     local[1].wait()
-    wo_c = []
-    for copy in wo_b:
-        copy.wait_recv()
-    for kf in range(1, F):
-        here = r.wo_ref.at[span((lower("f", kf) * 2 + c) * half, half), :]
-        wo_c.append(start(here, here, sibling))
     for copy in wo_c:
         copy.wait_recv()
     squares = jnp.zeros((tok, 1), F32)
@@ -1262,6 +1295,7 @@
 
         columns(shard, hidden_cols)
 
+    def back_part(kf):
         def back_cols(cols):
             r.back_s[kf, :, cols] = nt(r.dp_all[kf], r.up_ref[cols, :]).astype(BF)
 
@@ -1285,14 +1319,33 @@
 
     n_out = 128
 
+    r_d = shard // (A * B)
+
+    def down_rows(kf, place):
+        cols = span(place * r_d, r_d)
+        grad = tn(r.hid_all[kf, :, cols], r.cot_all[kf])
+        r.gd_ref[cols, :] = (grad + r.gd_ref[cols, :].astype(F32) if kf else grad).astype(BF)
+
     def down_grad(kf):
+        if kf < F - 1:
+
+            def rows_of(i, carry):
+                down_rows(kf, i)
+                return carry
+
+            lax.fori_loop(0, A * B, rows_of, 0)
+            return
+        for i in range(A):
+            for kb in range(1, B):
+                down_rows(kf, lax.rem(b + kb, B) * A + x.offset(x.order[i]))
+            x.send_down(i, i + 1)
+
+    def down_grad_own(kf):
         def rows_of(i, carry):
-            cols = span(i * n_out, n_out)
-            grad = tn(r.hid_all[kf, :, cols], r.cot_all[kf])
-            r.gd_ref[cols, :] = (grad + r.gd_ref[cols, :].astype(F32) if kf else grad).astype(BF)
+            down_rows(kf, b * A + i)
             return carry
 
-        lax.fori_loop(0, shard // n_out, rows_of, 0)
+        lax.fori_loop(0, A, rows_of, 0)
 
     def up_grad(kf):
         def rows_of(i, carry):
@@ -1308,20 +1361,22 @@
     back_copies, out_copies, back_back, out_back = [None] * F, [None] * F, [], []
     n2_c[0].wait_recv()
     cot_c[0].wait_recv()
-    back_copies[0] = feed_forward(0)
+    feed_forward(0)
+    back_copies[0] = back_part(0)
     down_grad(0)
     up_grad(0)
-    out_copies[0] = out_part(0)
     for kf in range(1, F):
         n2_f[kf - 1].wait_recv()
         n2_c.append(start(r.n2_all.at[kf, :tok], r.n2_all.at[kf, tok:], sibling))
     for kf in range(1, F):
         n2_c[kf].wait_recv()
         cot_c[kf].wait_recv()
-        back_copies[kf] = feed_forward(kf)
+        feed_forward(kf)
         if kf == F - 1:
             down_grad(kf)
-            x.send_down(0, A)
+        back_copies[kf] = back_part(kf)
+        if kf == F - 1:
+            down_grad_own(kf)
         back_copies[kf].wait_recv()
         chip_sum(kf, r.back_s, r.back_c, r.back_y)
         back_back.append(start(r.back_y.at[kf - 1], r.back_r.at[kf - 1], device("f", F - kf)))
@@ -1334,7 +1389,10 @@
         out_copies[kf].wait_recv()
         chip_sum(kf, r.out_s, r.out_c, r.out_y)
         out_back.append(start(r.out_y.at[kf - 1], r.out_r.at[kf - 1], device("f", F - kf)))
+    out_copies[0] = out_part(0)
     x.down_step(0)
+    if A > 2:
+        x.down_step(1)
 
     back_copies[0].wait_recv()
     for copy in back_back:
@@ -1372,7 +1430,7 @@
 
     lax.fori_loop(0, D // n_out, out_grad, 0)
     if A > 2:
-        x.down_step(1)
+        x.down_step(2)
 
     def finish_output():
         out_copies[0].wait_recv()

time: 236 us -> 224 us (0.949)
  Pallas kernels: 232 us -> 220 us
    pallas_call x1, Pallas kernels: 221 us -> 209 us  [layer(): pl.pallas_call(functools.partial(tail_kernel, dims, head, names), out_sha...]
where the time goes in v2:
time: 224 us
  Pallas kernels  220 us (98%)
    pallas_call x1, Pallas kernels, layer(): pl.pallas_call(functools.partial(tail_kernel, dims, head, names), out_sha...  209 us
    pallas_call x1, Pallas kernels, results(): pl.pallas_call(widen_kernel, grid=(steps,), out_shape=[jax.ShapeDtypeStru...  11.3 us

profile of v2, /device:TPU:0, one launch (start us, length us, event | category | flops | bytes accessed | tf_op | source)
XLA Modules:
  0.0 223.8 jit_solution(3080542066225597412)
XLA Ops:
  0.7 1.4 broadcast_select_fusion.refs_3_
  2.0 209.2 %layer.1 = (bf16[2048,1024]{1,0:T(8,128)(2,1)}, bf16[2,512,2048]{2,1,0:T(8,128)(2,1)}, bf16[512,1024]{1,0:T(8,128)(2,1)}, bf16[512,1024]{1,0:T(8,128)(2,1)}, bf1...) custom-call(s32[2,3]{1,0:T(2,128)} %refs_0_.1, s32[2]{0:T(128)} %refs_1_.1, ...), custom_call_target="tpu_custom_call" | custom-call | flops 34359738368 | bytes 33554432 | tf_op jit(solution)/shard_map/layer/pallas_call | solution.py:1550
  211.2 11.3 %widen.1 = (bf16[1,256,1024]{2,1,0:T(8,128)(2,1)}, f32[1,256,1024]{2,1,0:T(8,128)}, f32[2048,1024]{1,0:T(8,128)}, f32[512,4096]{1,0:T(8,128)}, f32[512,1024]{1,0...) custom-call(bf16[256,1024]{1,0:T(8,128)(2,1)} %get-tuple-element.26.low_ref, ...), custom_call_target="tpu_custom_call" | custom-call | tf_op jit(solution)/shard_map/widen/pallas_call | solution.py:1846
  222.5 1.3 slice_bitcast_fusion
  (1 shorter events, 0.0 us)

commit v3 on v2

--- a/solution.py
+++ b/solution.py
@@ -637,6 +637,8 @@
         if masked:
             at = j * CHUNK + lax.broadcasted_iota(jnp.int32, (CHUNK, tok), 0)
             mask = jnp.logical_and(at >= begin, at <= pos)
+        else:
+            seen = begin <= j * CHUNK
         d_keys = jnp.zeros((CHUNK, HS), F32)
         d_values = jnp.zeros((CHUNK, HS), F32)
         for h in range(H):
@@ -646,7 +648,10 @@
             scores = nt(keys, q)
             if masked:
                 scores = jnp.where(mask, scores, NEG)
-            probs = jnp.exp2(scores * factor - lse_ref[h : h + 1, :])
+            lse = lse_ref[h : h + 1, :]
+            if not masked:
+                lse = jnp.where(seen, lse, 3e38)
+            probs = jnp.exp2(scores * factor - lse)
             d_probs = nt(values, d)
             d_scores = (probs * (d_probs - delta[h : h + 1, :])).astype(BF)
             d_values = d_values + nn(probs.astype(BF), d)
@@ -659,7 +664,7 @@
 
     chunks = s // 2 + 1
     def attention_chunk(j, carry):
-        plain = jnp.logical_and(jnp.logical_and(j > 0, j < chunks - 1), s < 2 * A * B - 1)
+        plain = jnp.logical_and(j > 0, j < chunks - 1)
 
         @pl.when(plain)
         def _():
@@ -673,21 +678,19 @@
 
     first = 0 if head is None else min(3, A - 1)
     steps = [functools.partial(down_step, i) for i in range(first, A - 1)]
-    steps += [functools.partial(up_step, i) for i in range(A - 2)] + [down_share, square_o.over_b]
-    if A == 4:
-        times = (3, 5, 6, 7) if head is not None else (0, 1, 2, 3, 4, 5, 6)
-        at_chunk = dict(zip(times, steps))
-        at_chunk[2 if head is not None else 7] = square_o.over_f
+    steps += [functools.partial(up_step, i) for i in range(A - 2)] + [down_share, functools.partial(up_step, A - 2), square_o.over_b]
+    if A == 4 and head is not None:
+        acts = [(1, steps[0]), (3, steps[1]), (4, steps[2]), (5, steps[4]), (2, square_o.over_f)]
     else:
-        at_chunk = {0: square_o.over_f, 1: lambda: [step() for step in steps]}
+        acts = [(0, square_o.over_f), *((1, act) for act in steps)]
 
     def chunk_and_step(j, carry):
         @pl.when(j < chunks)
         def _():
             attention_chunk(j, 0)
 
-        for time, act in at_chunk.items():
-            pl.when(j == time)(lambda act=act: act() and None)
+        for time, act in acts:
+            pl.when(j == time)(act)
         return carry
 
     lax.fori_loop(0, window // CHUNK, chunk_and_step, 0)
@@ -730,7 +733,8 @@
         for j in range(A):
             x_kv.append(start(dkv_c.at[j * B + other], dkv_x.at[kb, j], slots(), device("b", kb + 1)))
 
-    up_step(A - 2)
+    if A == 4 and head is not None:
+        steps[3]()
     square_q.over_f()
     gather_down.from_a((0,))
     up_share()
@@ -751,7 +755,7 @@
 
     lax.fori_loop(0, A, add_x, 0)
     z_kv = slots(A - 1)
-    for k in range(1, A):
+    for k in range(A - 1, 0, -1):
 
         @pl.when(a - k >= 0)
         def _():
@@ -1009,7 +1013,6 @@
     gains_f = to_f(lambda kf: r.gains_in, lambda kf: r.gains_all.at[f])
     wk_f = to_f(lambda kf: r.wk_in.at[mine_half, :], lambda kf: r.wkv_ref.at[full_half, :HS])
     wv_f = to_f(lambda kf: r.wv_in.at[mine_half, :], lambda kf: r.wkv_ref.at[full_half, HS:])
-    wq_f = to_f(lambda kf: r.wq_in.at[mine_half, :], lambda kf: r.wq_ref.at[full_half, :])
     part, up_part = half // B, own_rows // B
 
     def wo_rows(f_, c_, b_):
@@ -1018,6 +1021,7 @@
     def up_rows(f_, b_):
         return span((f_ * B + b_) * up_part, up_part)
 
+    wq_f = to_f(lambda kf: r.wq_in.at[span((c * B + b) * part, part), :], lambda kf: r.wq_ref.at[wo_rows(f, c, b), :])
     wo_f = to_f(lambda kf: r.wo_in.at[span((c * B + b) * part, part), :], lambda kf: r.wo_ref.at[wo_rows(f, c, b), :])
     up_f = to_f(
         lambda kf: r.up_in.at[span(b * up_part, up_part), span((lax.rem(f + kf, F) * 2 + c) * shard, shard)],
@@ -1131,11 +1135,17 @@
         z_copies[k - 1].wait_recv()
         pass_on(k)
 
+    wq_b = along_b(wq_f, r.wq_ref, lambda f_: wo_rows(f_, c, b))
     if A > 2:
         guarded(1, a >= 1, functools.partial(from_a, 1))
 
     local[0].wait()
-    wq_c = weight_halves(wq_f, r.wq_ref, slice(0, D))
+    for copy in wq_b:
+        copy.wait_recv()
+    wq_c = []
+    for kf in range(1, F):
+        here = r.wq_ref.at[span((lower("f", kf) * 2 + c) * half, half), :]
+        wq_c.append(start(here, here, sibling))
     for copy in wq_c:
         copy.wait_recv()
     n_cols = 256
@@ -1173,6 +1183,8 @@
         if masked:
             at = j * CHUNK + lax.broadcasted_iota(jnp.int32, (tok, CHUNK), 1)
             mask = jnp.logical_and(at >= begin, at <= pos)
+        else:
+            seen = begin <= j * CHUNK
         for h in range(H):
             cols = slice(h * HS, (h + 1) * HS)
             scores = nt(r.q_ref[:, cols], keys)
@@ -1180,9 +1192,13 @@
                 scores = jnp.where(mask, scores, NEG)
             old = top[:, cols]
             new = jnp.maximum(old, jnp.max(scores, axis=1, keepdims=True) * factor)
+            if not masked:
+                new = jnp.where(seen, new, old)
             shrink = jnp.exp2(old - new)
             probs = jnp.exp2(scores * factor - jnp.concatenate([new] * (CHUNK // HS), axis=1))
             both = nn(probs.astype(BF), values)
+            if not masked:
+                both = jnp.where(seen, both, 0.0)
             mixed[:, cols] = mixed[:, cols] * shrink + both[:, :HS]
             total[:, cols] = total[:, cols] * shrink + both[:, HS:]
             top[:, cols] = new
@@ -1224,20 +1240,18 @@
     from_c(0)
 
     def begin_group(k):
-        for later in range(2, A) if k == 1 else ():
-            guarded(later, a - later >= 0, functools.partial(from_b, later))
+        if k + 1 < A:
+            guarded(k + 1, a - (k + 1) >= 0, functools.partial(from_b, k + 1))
         from_c(k)
-        if k == 2:
+        if k == A - 1:
             pass_weights()
 
     def attention_chunk(j, carry):
-        plain = jnp.logical_and(j > 0, s < 2 * A * B - 1)
-
-        @pl.when(plain)
+        @pl.when(j > 0)
         def _():
             step(j, False)
 
-        @pl.when(jnp.logical_not(plain))
+        @pl.when(j == 0)
         def _():
             step(j, True)
 
@@ -1250,7 +1264,7 @@
         return attention_chunk(j, carry)
 
     lax.fori_loop(0, last, attention_part, 0)
-    guarded(1, a < 2, pass_weights)
+    guarded(1, a < A - 1, pass_weights)
     for h in range(H):
         cols = slice(h * HS, (h + 1) * HS)
         r.att_ref[:, cols] = (mixed[:, cols] * (1.0 / total[:, cols])).astype(BF)
@@ -1321,39 +1335,33 @@
 
     r_d = shard // (A * B)
 
-    def down_rows(kf, place):
+    def down_rows(kfs, place):
         cols = span(place * r_d, r_d)
-        grad = tn(r.hid_all[kf, :, cols], r.cot_all[kf])
-        r.gd_ref[cols, :] = (grad + r.gd_ref[cols, :].astype(F32) if kf else grad).astype(BF)
+        grad = sum(tn(r.hid_all[kf, :, cols], r.cot_all[kf]) for kf in kfs)
+        if 0 not in kfs:
+            grad = grad + r.gd_ref[cols, :].astype(F32)
+        r.gd_ref[cols, :] = grad.astype(BF)
 
     def down_grad(kf):
-        if kf < F - 1:
-
-            def rows_of(i, carry):
-                down_rows(kf, i)
-                return carry
-
-            lax.fori_loop(0, A * B, rows_of, 0)
-            return
         for i in range(A):
             for kb in range(1, B):
-                down_rows(kf, lax.rem(b + kb, B) * A + x.offset(x.order[i]))
-            x.send_down(i, i + 1)
-
-    def down_grad_own(kf):
+                down_rows((kf,), lax.rem(b + kb, B) * A + x.offset(x.order[i]))
+            if kf == F - 1:
+                x.send_down(i, i + 1)
+
+    def down_grad_own():
         def rows_of(i, carry):
-            down_rows(kf, b * A + i)
+            down_rows(range(F), b * A + i)
             return carry
 
         lax.fori_loop(0, A, rows_of, 0)
 
-    def up_grad(kf):
+    def up_grad():
         def rows_of(i, carry):
             cols = span(i * n_out, n_out)
             rows = span(lax.rem(i, own_rows // n_out) * n_out, n_out)
-            at = i // (own_rows // n_out)
-            grad = tn(r.n2_all[kf, :, cols], r.dp_all[kf])
-            r.gu_ref[at, rows, :] = (grad + r.gu_ref[at, rows, :].astype(F32) if kf else grad).astype(BF)
+            grad = sum(tn(r.n2_all[kf, :, cols], r.dp_all[kf]) for kf in range(F))
+            r.gu_ref[i // (own_rows // n_out), rows, :] = grad.astype(BF)
             return carry
 
         lax.fori_loop(0, D // n_out, rows_of, 0)
@@ -1362,9 +1370,8 @@
     n2_c[0].wait_recv()
     cot_c[0].wait_recv()
     feed_forward(0)
+    down_grad(0)
     back_copies[0] = back_part(0)
-    down_grad(0)
-    up_grad(0)
     for kf in range(1, F):
         n2_f[kf - 1].wait_recv()
         n2_c.append(start(r.n2_all.at[kf, :tok], r.n2_all.at[kf, tok:], sibling))
@@ -1372,27 +1379,27 @@
         n2_c[kf].wait_recv()
         cot_c[kf].wait_recv()
         feed_forward(kf)
-        if kf == F - 1:
-            down_grad(kf)
+        down_grad(kf)
         back_copies[kf] = back_part(kf)
         if kf == F - 1:
-            down_grad_own(kf)
+            down_grad_own()
         back_copies[kf].wait_recv()
         chip_sum(kf, r.back_s, r.back_c, r.back_y)
         back_back.append(start(r.back_y.at[kf - 1], r.back_r.at[kf - 1], device("f", F - kf)))
-        if kf < F - 1:
-            down_grad(kf)
-        up_grad(kf)
+        if kf == F - 1:
+            up_grad()
+            x.send_up(0, A)
+            x.down_step(0)
         out_copies[kf] = out_part(kf)
-    x.send_up(0, A)
     for kf in range(1, F):
         out_copies[kf].wait_recv()
         chip_sum(kf, r.out_s, r.out_c, r.out_y)
         out_back.append(start(r.out_y.at[kf - 1], r.out_r.at[kf - 1], device("f", F - kf)))
-    out_copies[0] = out_part(0)
-    x.down_step(0)
     if A > 2:
         x.down_step(1)
+    out_copies[0] = out_part(0)
+    if A > 2:
+        x.down_step(2)
 
     back_copies[0].wait_recv()
     for copy in back_back:
@@ -1429,8 +1436,6 @@
         return carry
 
     lax.fori_loop(0, D // n_out, out_grad, 0)
-    if A > 2:
-        x.down_step(2)
 
     def finish_output():
         out_copies[0].wait_recv()

time: 224 us -> 216 us (0.964)
  Pallas kernels: 220 us -> 212 us
    pallas_call x1, Pallas kernels: 209 us -> 200 us  [layer(): pl.pallas_call(functools.partial(tail_kernel, dims, head, names), out_sha...]
where the time goes in v3:
time: 216 us; the launch traced here: 215 us
  Pallas kernels  212 us (98%)
    pallas_call x1, Pallas kernels, layer(): pl.pallas_call(functools.partial(tail_kernel, dims, head, names), out_sha...  200 us
    pallas_call x1, Pallas kernels, results(): pl.pallas_call(widen_kernel, grid=(steps,), out_shape=[jax.ShapeDtypeStru...  11.3 us

profile of v3, /device:TPU:0, one launch (start us, length us, event | category | flops | bytes accessed | tf_op | source)
XLA Modules:
  0.0 214.9 jit_solution(4387828683425039002)
XLA Ops:
  0.7 1.4 broadcast_select_fusion.refs_3_
  2.0 200.3 %layer.1 = (bf16[2048,1024]{1,0:T(8,128)(2,1)}, bf16[2,512,2048]{2,1,0:T(8,128)(2,1)}, bf16[512,1024]{1,0:T(8,128)(2,1)}, bf16[512,1024]{1,0:T(8,128)(2,1)}, bf1...) custom-call(s32[2,3]{1,0:T(2,128)} %refs_0_.1, s32[2]{0:T(128)} %refs_1_.1, ...), custom_call_target="tpu_custom_call" | custom-call | flops 34359738368 | bytes 33554432 | tf_op jit(solution)/shard_map/layer/pallas_call | solution.py:1555
  202.3 11.3 %widen.1 = (bf16[1,256,1024]{2,1,0:T(8,128)(2,1)}, f32[1,256,1024]{2,1,0:T(8,128)}, f32[2048,1024]{1,0:T(8,128)}, f32[512,4096]{1,0:T(8,128)}, f32[512,1024]{1,0...) custom-call(bf16[256,1024]{1,0:T(8,128)(2,1)} %get-tuple-element.26.low_ref, ...), custom_call_target="tpu_custom_call" | custom-call | tf_op jit(solution)/shard_map/widen/pallas_call | solution.py:1851
  213.6 1.3 slice_bitcast_fusion
  (1 shorter events, 0.0 us)

commit v4 on v3

--- a/solution.py
+++ b/solution.py
@@ -932,7 +932,8 @@
     "lengths",
     "groups",
     "tokens",
-    "gains_in",
+    "gain_a_in",
+    "gain_f_in",
     "wk_in",
     "wv_in",
     "cot_in",
@@ -1010,7 +1011,10 @@
     def to_f(src, dst):
         return [start(src(kf), dst(kf), device("f", kf)) for kf in range(1, F)]
 
-    gains_f = to_f(lambda kf: r.gains_in, lambda kf: r.gains_all.at[f])
+    row = lax.broadcasted_iota(jnp.int32, (16, own_rows), 0)
+    both = [ref[...].astype(F32).reshape(1, own_rows) for ref in (r.gain_a_in, r.gain_f_in)]
+    r.gains_all[f] = jnp.where(row == 0, *both).astype(BF)
+    gains_f = to_f(lambda kf: r.gains_all.at[f], lambda kf: r.gains_all.at[f])
     wk_f = to_f(lambda kf: r.wk_in.at[mine_half, :], lambda kf: r.wkv_ref.at[full_half, :HS])
     wv_f = to_f(lambda kf: r.wv_in.at[mine_half, :], lambda kf: r.wkv_ref.at[full_half, HS:])
     part, up_part = half // B, own_rows // B
@@ -1078,7 +1082,6 @@
     lax.fori_loop(0, tok // n_rows, unit_rows, 0)
     r.wkv_ref[mine, :HS] = r.wk_in[...]
     r.wkv_ref[mine, HS:] = r.wv_in[...]
-    r.gains_all[f] = r.gains_in[...]
     for copy in gains_f:
         copy.wait_recv()
     for i in range(F):
@@ -1548,20 +1551,20 @@
     return total
 
 
-def layer(dims, lengths, groups, tokens, gains, w_key, w_value, cotangent, w_query, w_out, w_up, w_down, outs, scratch):
+def layer(dims, lengths, groups, tokens, gain_a, gain_f, w_key, w_value, cotangent, w_query, w_out, w_up, w_down, outs, scratch):
     tok, D = tokens.shape
     hbm = pl.BlockSpec(memory_space=pltpu.HBM)
     names = HEAD_IN + TAIL_OUT[:5] + ("grad_hbm", "out_hbm") + HEAD_SCRATCH + tuple(n for n in TAIL_SCRATCH if n not in AGAIN)
     return pl.pallas_call(
         functools.partial(tail_kernel, dims, head, names),
         out_shape=outs,
-        in_specs=[SMEM] * 2 + [VMEM] * 4 + [hbm] * 5,
+        in_specs=[SMEM] * 2 + [VMEM] * 5 + [hbm] * 5,
         out_specs=(hbm,) * 7,
         scratch_shapes=scratch,
         compiler_params=pltpu.CompilerParams(vmem_limit_bytes=LIMIT, collective_id=2, has_side_effects=True),
         cost_estimate=pl.CostEstimate(flops=2**35, bytes_accessed=2**25, transcendentals=2**24),
         name="layer",
-    )(lengths, groups, tokens, gains, w_key, w_value, cotangent, w_query, w_out, w_up, w_down)
+    )(lengths, groups, tokens, gain_a, gain_f, w_key, w_value, cotangent, w_query, w_out, w_up, w_down)
 
 
 def after(value, *others):
@@ -1661,14 +1664,13 @@
 
     outs, scratch, fits = layer_shapes((A, B, F), tok, D, shard, seq_parts * tok, seq_lengths.shape[1])
     if fits:
-        row = lax.broadcasted_iota(jnp.int32, (16, own_rows), 0)
-        gains = jnp.where(row == 0, gain_attn[None], gain_ffn[None])
         *grads, grad_tokens, output = layer(
             (A, B, F),
             seq_lengths,
             group_of_shard,
             tokens[0],
-            gains,
+            gain_attn,
+            gain_ffn,
             w_key,
             w_value,
             cotangent[0],
@@ -1811,7 +1813,7 @@
 
 
 def widen_kernel(
-    low_ref, grad_ref, down_ref, up_ref, o_ref, q_ref, kv_ref, output, grad_tokens, grad_down, grad_up, grad_o, grad_q, grad_k, grad_v, gains
+    low_ref, grad_ref, down_ref, up_ref, o_ref, q_ref, kv_ref, output, grad_tokens, grad_down, grad_up, grad_o, grad_q, grad_k, grad_v, gain_a, gain_f
 ):
     output[0] = low_ref[...]
     grad_tokens[0] = grad_ref[...]
@@ -1828,8 +1830,10 @@
         for i in range(kv_ref.shape[1]):
             grad_k[i * rows : (i + 1) * rows, :] = kv_ref[0, i, :rows, :].astype(F32)
             grad_v[i * rows : (i + 1) * rows, :] = kv_ref[1, i, :rows, :].astype(F32)
-        for i in range(2):
-            gains[i] = kv_ref[i, 0, rows:, :].astype(F32)
+        for i, gain in enumerate((gain_a, gain_f)):
+            block = kv_ref[i, 0, rows:, :].astype(F32)
+            for k in range(gain.shape[0] // HS):
+                gain[k * HS : (k + 1) * HS] = block[k]
 
 
 def results(output, grad_tokens, down_all, up_all, out_all, query_all, kv_all):
@@ -1847,8 +1851,8 @@
         return pl.BlockSpec((1, n // steps, cols), lambda i: (0, i, 0))
 
     down_rows = down_all.shape[0]
-    shapes = [(down_rows, D), (own_rows, F * width), (own_rows, D), (own_rows, D), (own_rows, HS), (own_rows, HS), (2, 16, HS)]
-    out, grad_tokens, down, up, o, q, k, v, gains = pl.pallas_call(
+    shapes = [(down_rows, D), (own_rows, F * width), (own_rows, D), (own_rows, D), (own_rows, HS), (own_rows, HS), (own_rows,), (own_rows,)]
+    out, grad_tokens, down, up, o, q, k, v, gain_a, gain_f = pl.pallas_call(
         widen_kernel,
         grid=(steps,),
         out_shape=[jax.ShapeDtypeStruct((1, tok, D), BF), jax.ShapeDtypeStruct((1, tok, D), F32)]
@@ -1871,13 +1875,13 @@
             rows(own_rows, D),
             whole(own_rows, HS),
             whole(own_rows, HS),
-            whole(2, 16, HS),
+            whole(own_rows),
+            whole(own_rows),
         ],
         compiler_params=pltpu.CompilerParams(vmem_limit_bytes=LIMIT),
         name="widen",
     )(output, grad_tokens, down_all, up_all, out_all, query_all, kv_all)
-    gains = gains[:, : own_rows // HS].reshape(2, own_rows)
-    return out, grad_tokens, gains[0], q, k, v, o, gains[1], up, down
+    return out, grad_tokens, gain_a, q, k, v, o, gain_f, up, down
 
 
 def solution(mesh):

time: 216 us -> 214 us (level)
  no operation moved by 1% of the time
where the time goes in v4:
time: 214 us; the launch traced here: 213 us
  Pallas kernels  212 us (99%)
    pallas_call x1, Pallas kernels, layer(): pl.pallas_call(functools.partial(tail_kernel, dims, head, names), out_sha...  201 us
    pallas_call x1, Pallas kernels, results(): pl.pallas_call(widen_kernel, grid=(steps,), out_shape=[jax.ShapeDtypeStru...  11.3 us

profile of v4, /device:TPU:0, one launch (start us, length us, event | category | flops | bytes accessed | tf_op | source)
XLA Modules:
  0.0 212.7 jit_solution(7160257467091978346)
XLA Ops:
  0.6 200.5 %layer.1 = (bf16[2048,1024]{1,0:T(8,128)(2,1)}, bf16[2,512,2048]{2,1,0:T(8,128)(2,1)}, bf16[512,1024]{1,0:T(8,128)(2,1)}, bf16[512,1024]{1,0:T(8,128)(2,1)}, bf1...) custom-call(s32[2,3]{1,0:T(2,128)} %refs_0_.1, s32[2]{0:T(128)} %refs_1_.1, ...), custom_call_target="tpu_custom_call" | custom-call | flops 34359738368 | bytes 33554432 | tf_op jit(solution)/shard_map/layer/pallas_call | solution.py:1558
  201.2 11.3 %widen.1 = (bf16[1,256,1024]{2,1,0:T(8,128)(2,1)}, f32[1,256,1024]{2,1,0:T(8,128)}, f32[2048,1024]{1,0:T(8,128)}, f32[512,4096]{1,0:T(8,128)}, f32[512,1024]{1,0...) custom-call(bf16[256,1024]{1,0:T(8,128)(2,1)} %get-tuple-element.27.l, ...), custom_call_target="tpu_custom_call" | custom-call | tf_op jit(solution)/shard_map/widen/pallas_call | solution.py:1855

commit v5 on v4

--- a/solution.py
+++ b/solution.py
@@ -544,7 +544,7 @@
             A=A, B=B, F=F, a=a, b=b, c=c, f=f, s=s, slots=slots, remote=remote, device=device, lower=lower,
             send_down=send_down, send_up=send_up, down_step=down_step, offset=offset, order=order,
         )
-        finish_output, finish_head = head(r, own)
+        finish_output, send_tokens, finish_head = head(r, own)
 
     def reduce_y(ref, got, sent, width):
         mine = pl.ds(pl.multiple_of(c * width, width), width)
@@ -813,6 +813,8 @@
         grad_tokens[:, cols] = dres_ref[:, cols] + inv_ref[...] * (
             dn1[:, cols] * gain_ref[:, cols] - tok_ref[:, cols].astype(F32) * inv_ref[...] * mean
         )
+    if head is not None:
+        send_tokens()
     kv_c_copy.wait()
     kv_c[...] = (kv_c[...].astype(F32) + gkv_ref[c].astype(F32)).astype(BF)
     kv_f = [start(kv_c.at[lax.rem(f + kf + 1, F)], kv_y.at[kf], slots(), device("f", kf + 1)) for kf in range(F - 1)]
@@ -1463,7 +1465,6 @@
     ]
 
     def finish():
-        results[1].start()
         for copy in results:
             copy.wait()
         for copy in sent:
@@ -1476,7 +1477,7 @@
                     guarded(k, a - k >= 0, x_copy(kb, k).wait_send)
                 guarded(k, a - k >= 0, c_copy(kb, k).wait_send)
 
-    return finish_output, finish
+    return finish_output, results[1].start, finish
 
 
 AGAIN = {

time: 214 us -> 213 us (level)
  no operation moved by 1% of the time
where the time goes in v5:
time: 213 us; the launch traced here: 212 us
  Pallas kernels  211 us (99%)
    pallas_call x1, Pallas kernels, layer(): pl.pallas_call(functools.partial(tail_kernel, dims, head, names), out_sha...  200 us
    pallas_call x1, Pallas kernels, results(): pl.pallas_call(widen_kernel, grid=(steps,), out_shape=[jax.ShapeDtypeStru...  11.3 us

profile of v5, /device:TPU:0, one launch (start us, length us, event | category | flops | bytes accessed | tf_op | source)
XLA Modules:
  0.0 211.7 jit_solution(317322032953894992)
XLA Ops:
  0.6 199.6 %layer.1 = (bf16[2048,1024]{1,0:T(8,128)(2,1)}, bf16[2,512,2048]{2,1,0:T(8,128)(2,1)}, bf16[512,1024]{1,0:T(8,128)(2,1)}, bf16[512,1024]{1,0:T(8,128)(2,1)}, bf1...) custom-call(s32[2,3]{1,0:T(2,128)} %refs_0_.1, s32[2]{0:T(128)} %refs_1_.1, ...), custom_call_target="tpu_custom_call" | custom-call | flops 34359738368 | bytes 33554432 | tf_op jit(solution)/shard_map/layer/pallas_call | solution.py:1559
  200.2 11.3 %widen.1 = (bf16[1,256,1024]{2,1,0:T(8,128)(2,1)}, f32[1,256,1024]{2,1,0:T(8,128)}, f32[2048,1024]{1,0:T(8,128)}, f32[512,4096]{1,0:T(8,128)}, f32[512,1024]{1,0...) custom-call(bf16[256,1024]{1,0:T(8,128)(2,1)} %get-tuple-element.27.l, ...), custom_call_target="tpu_custom_call" | custom-call | tf_op jit(solution)/shard_map/widen/pallas_call | solution.py:1856
